TPU v7x, 32 devices: a whole 2x2x4 slice. The times are simulated.
32 devices in a mesh: expert: 4 (over x, core), shard: 8 (over z, y).
Axes of the slice: x: 2, y: 2, z: 4, core: 2. Of those that a mesh axis runs over, the one named last changes fastest.
Arguments:
- tokens: bfloat16 [8, 1024, 1024], P('shard', 'expert'), may hold values from -6 to 6
- cotangent: bfloat16 [8, 1024, 1024], P('shard', 'expert'), may hold values from -6 to 6
- routes: int32 [8, 1024, 8], P('shard', 'expert'), may hold values from 0 to 15, all different within a row; in each aligned block of 256 rows (0 to 255, 256 to 511, ..., all dimensions but the last counted through in order) at most 136 rows name the same one
- qkv_w: float32 [1024, 2048], P('shard'), may hold values from -0.1875 to 0.1875
- qkv_m: float32 [1024, 2048], P('shard'), may hold values from -48 to 48
- qkv_v: float32 [1024, 2048], P('shard'), may hold values from 294.912 to 1179.648
- out_w: float32 [1024, 1024], P('shard'), may hold values from -2 to 2
- out_m: float32 [1024, 1024], P('shard'), may hold values from -4 to 4
- out_v: float32 [1024, 1024], P('shard'), may hold values from 2.32 to 9.2
- router_w: float32 [1024, 16], P('shard'), may hold values from -0.09375 to 0.09375
- router_m: float32 [1024, 16], P('shard'), may hold values from -384 to 384
- router_v: float32 [1024, 16], P('shard'), may hold values from 19660.8 to 78643.2
- gains: float32 [2, 1024], P(None, 'shard'), may hold values from 0.5 to 1.5
- gains_m: float32 [2, 1024], P(None, 'shard'), may hold values from -80 to 80
- gains_v: float32 [2, 1024], P(None, 'shard'), may hold values from 737.28 to 2949.12
- expert_in: float32 [16, 2, 512, 1024], P('expert', None, 'shard'), may hold values from -0.1875 to 0.1875
- in_m: float32 [16, 2, 512, 1024], P('expert', None, 'shard'), may hold values from -16 to 16
- in_v: float32 [16, 2, 512, 1024], P('expert', None, 'shard'), may hold values from 38.4 to 153.6
- expert_out: float32 [16, 512, 1024], P('expert', 'shard'), may hold values from -1 to 1
- down_m: float32 [16, 512, 1024], P('expert', 'shard'), may hold values from -3 to 3
- down_v: float32 [16, 512, 1024], P('expert', 'shard'), may hold values from 1.216 to 4.864
Outputs:
- output: bfloat16 [8, 1024, 1024], P('shard', 'expert')
- input_grad: float32 [8, 1024, 1024], P('shard', 'expert')
- qkv_m_new: float32 [1024, 2048], P('shard')
- qkv_v_new: float32 [1024, 2048], P('shard')
- qkv_w_new: float32 [1024, 2048], P('shard')
- out_m_new: float32 [1024, 1024], P('shard')
- out_v_new: float32 [1024, 1024], P('shard')
- out_w_new: float32 [1024, 1024], P('shard')
- router_m_new: float32 [1024, 16], P('shard')
- router_v_new: float32 [1024, 16], P('shard')
- router_w_new: float32 [1024, 16], P('shard')
- gains_m_new: float32 [2, 1024], P(None, 'shard')
- gains_v_new: float32 [2, 1024], P(None, 'shard')
- gains_new: float32 [2, 1024], P(None, 'shard')
- in_m_new: float32 [16, 2, 512, 1024], P('expert', None, 'shard')
- in_v_new: float32 [16, 2, 512, 1024], P('expert', None, 'shard')
- expert_in_new: float32 [16, 2, 512, 1024], P('expert', None, 'shard')
- down_m_new: float32 [16, 512, 1024], P('expert', 'shard')
- down_v_new: float32 [16, 512, 1024], P('expert', 'shard')
- expert_out_new: float32 [16, 512, 1024], P('expert', 'shard')
Inputs may be any that keep to these rules, and one draw needn't show every extreme that they name: `routes`: each token names 8 different experts. Among the tokens of one device no expert is named more than 136 times, a bound that some block reaches.
All inputs are finite; a program needn't handle non-finite values.
Results may differ from a plain program's by a relative error of at most 0.028.
Values may be sent and summed in bfloat16 or wider, within the bound.
No kernel may reach another device: no remote copies, remote signals or barrier semaphores. Data moves between devices by JAX's collectives and lax.ppermute only.
A program may use at most 256 MiB of HBM per device.

v0:
```python
import jax
import jax.numpy as jnp
from jax import lax
from jax.sharding import PartitionSpec as P

D = 1024
HQ = 16
KVH = 8
HD = 64
FF = 512
STEP = 10


beta_one = 0.9
beta_two = 0.95
adam_eps = 1e-08
weight_decay = 0.1
norm_eps = 1e-05
rope_base = 10000.0
masked_score = -1e30


def rms_scale(values):
    return lax.rsqrt(jnp.mean(values * values, axis=-1, keepdims=True) + norm_eps)


def norm_back(values, scale, gain, grad):
    weighted = gain * grad
    inner = jnp.mean(values * weighted, axis=-1, keepdims=True)
    return scale * weighted - values * (scale * scale * scale) * inner


def rotary(values, positions, sign):
    half = values.shape[-1] // 2
    freqs = rope_base ** (-jnp.arange(half, dtype=jnp.float32) / half)
    angles = positions.astype(jnp.float32)[:, None] * freqs[None, :]
    cosine = jnp.cos(angles)[:, None, :]
    sine = sign * jnp.sin(angles)[:, None, :]
    first = values[..., :half]
    second = values[..., half:]
    return jnp.concatenate(
        [first * cosine - second * sine, second * cosine + first * sine], axis=-1
    )


def slot_index(route_rows, experts, capacity):
    flat_routes = route_rows.reshape(-1)
    onehot = (flat_routes[:, None] == jnp.arange(experts, dtype=jnp.int32)[None, :]).astype(
        jnp.int32
    )
    counts = jnp.cumsum(onehot, axis=0)
    slot = jnp.sum(counts * onehot, axis=1) - 1
    return (flat_routes * capacity + slot).reshape(route_rows.shape)


def adam_step(weight, first, second, grad, rate, decay):
    new_first = beta_one * first + (1.0 - beta_one) * grad
    new_second = beta_two * second + (1.0 - beta_two) * grad * grad
    fix_one = 1.0 - beta_one**STEP
    fix_two = 1.0 - beta_two**STEP
    update = new_first / fix_one / (jnp.sqrt(new_second / fix_two) + adam_eps)
    return (new_first, new_second, weight - rate * (update + decay * weight))


def body(
    tokens,
    cotangent,
    routes,
    qkv_w,
    qkv_m,
    qkv_v,
    out_w,
    out_m,
    out_v,
    router_w,
    router_m,
    router_v,
    gains,
    gains_m,
    gains_v,
    expert_in,
    in_m,
    in_v,
    expert_out,
    down_m,
    down_v,
):
    rows = tokens.shape[1]
    width = tokens.shape[2]
    spread = lax.axis_size("expert")
    length = rows * spread
    top = routes.shape[2]
    experts = router_w.shape[1]
    owned = expert_in.shape[0]
    capacity = rows * top * 17 // (experts * 16)
    heads_dim = HQ * HD
    kv_dim = KVH * HD
    repeat = HQ // KVH
    qkv_all, out_all, router_all, gains_all = (
        lax.all_gather(qkv_w.astype(jnp.bfloat16), "shard", axis=0, tiled=True),
        lax.all_gather(out_w.astype(jnp.bfloat16), "shard", axis=0, tiled=True),
        lax.all_gather(router_w.astype(jnp.bfloat16), "shard", axis=0, tiled=True),
        lax.all_gather(gains.astype(jnp.bfloat16), "shard", axis=1, tiled=True),
    )
    in_all, down_all = (
        lax.all_gather(expert_in.astype(jnp.bfloat16), "shard", axis=2, tiled=True),
        lax.all_gather(expert_out.astype(jnp.bfloat16), "shard", axis=1, tiled=True),
    )
    in_flat = in_all.reshape(owned, 2 * FF, width)
    gain_one = gains_all[0].astype(jnp.float32)
    gain_two = gains_all[1].astype(jnp.float32)
    inputs = tokens[0].astype(jnp.float32)
    scale_one = rms_scale(inputs)
    norm_one = (inputs * scale_one * gain_one).astype(jnp.bfloat16)
    proj = jnp.dot(norm_one, qkv_all, preferred_element_type=jnp.float32)
    positions = lax.axis_index("expert") * rows + jnp.arange(rows, dtype=jnp.int32)
    query = rotary(proj[:, :heads_dim].reshape(rows, HQ, HD), positions, 1.0).astype(jnp.bfloat16)
    key = rotary(
        proj[:, heads_dim : heads_dim + kv_dim].reshape(rows, KVH, HD), positions, 1.0
    ).astype(jnp.bfloat16)
    value = proj[:, heads_dim + kv_dim :].astype(jnp.bfloat16)
    keys_all, values_all = (
        lax.all_gather(key.reshape(rows, kv_dim), "expert", axis=0, tiled=True),
        lax.all_gather(value, "expert", axis=0, tiled=True),
    )
    query4 = query.reshape(rows, KVH, repeat, HD)
    key3 = keys_all.reshape(length, KVH, HD)
    value3 = values_all.reshape(length, KVH, HD)
    causal = jnp.arange(length, dtype=jnp.int32)[None, :] <= positions[:, None]

    def score_block():
        raw = jnp.einsum("qkrd,tkd->krqt", query4, key3, preferred_element_type=jnp.float32) * 0.125
        return jnp.where(causal, raw, masked_score)

    masked = score_block()
    peak = jnp.max(masked, axis=-1, keepdims=True)
    total = jnp.sum(jnp.exp(masked - peak), axis=-1, keepdims=True)
    log_total = peak + jnp.log(total)
    probs = jnp.exp(masked - log_total).astype(jnp.bfloat16)
    attended = jnp.einsum("krqt,tkd->qkrd", probs, value3, preferred_element_type=jnp.float32)
    attended = attended.reshape(rows, heads_dim).astype(jnp.bfloat16)
    middle = inputs + jnp.dot(attended, out_all, preferred_element_type=jnp.float32)
    scale_two = rms_scale(middle)
    norm_two = (middle * scale_two * gain_two).astype(jnp.bfloat16)
    logits = jnp.dot(norm_two, router_all, preferred_element_type=jnp.float32)
    route_rows = routes[0]
    chosen = route_rows[:, :, None] == jnp.arange(experts, dtype=jnp.int32)[None, None, :]
    selected = jnp.sum(jnp.where(chosen, logits[:, None, :], 0.0), axis=-1)
    gates = jax.nn.softmax(selected, axis=-1)
    flat = slot_index(route_rows, experts, capacity).reshape(-1)
    assign_count = rows * top
    source = (
        jnp.full((experts * capacity,), assign_count, jnp.int32)
        .at[flat]
        .set(jnp.arange(assign_count, dtype=jnp.int32))
    )
    padded_norm = jnp.concatenate([norm_two, jnp.zeros((1, width), jnp.bfloat16)], axis=0)
    sending = padded_norm[source // top].reshape(spread, owned, capacity, width)
    expert_rows = lax.all_to_all(sending, "expert", split_axis=0, concat_axis=2, tiled=True)[0]
    both = jnp.einsum("end,efd->enf", expert_rows, in_flat, preferred_element_type=jnp.float32)
    gate_part = both[..., :FF]
    up_part = both[..., FF:]
    active = (jax.nn.silu(gate_part) * up_part).astype(jnp.bfloat16)
    results = jnp.einsum(
        "enf,efd->end", active, down_all, preferred_element_type=jnp.float32
    ).astype(jnp.bfloat16)
    returned = lax.all_to_all(
        results[None], "expert", split_axis=2, concat_axis=0, tiled=True
    ).reshape(experts * capacity, width)
    picked = returned[flat].reshape(rows, top, width).astype(jnp.float32)
    output = (middle + jnp.sum(gates[:, :, None] * picked, axis=1)).astype(jnp.bfloat16)
    out_grad = cotangent[0].astype(jnp.float32)
    gate_grads = jnp.sum(out_grad[:, None, :] * picked, axis=-1)
    row_grads = (
        (gates[:, :, None] * out_grad[:, None, :]).astype(jnp.bfloat16).reshape(assign_count, width)
    )
    padded_grads = jnp.concatenate([row_grads, jnp.zeros((1, width), jnp.bfloat16)], axis=0)
    grad_sending = padded_grads[source].reshape(spread, owned, capacity, width)
    result_grads = lax.all_to_all(grad_sending, "expert", split_axis=0, concat_axis=2, tiled=True)[
        0
    ]
    down_grad = jnp.einsum("enf,end->efd", active, result_grads, preferred_element_type=jnp.float32)
    down_total = lax.psum_scatter(
        down_grad.astype(jnp.bfloat16), "shard", scatter_dimension=1, tiled=True
    ).astype(jnp.float32)
    active_grad = jnp.einsum(
        "end,efd->enf", result_grads, down_all, preferred_element_type=jnp.float32
    )
    sigmoid = jax.nn.sigmoid(gate_part)
    gate_grad = active_grad * up_part * sigmoid * (1.0 + gate_part * (1.0 - sigmoid))
    up_grad = active_grad * gate_part * sigmoid
    both_grad = jnp.concatenate([gate_grad, up_grad], axis=-1).astype(jnp.bfloat16)
    in_grad = jnp.einsum(
        "enf,end->efd", both_grad, expert_rows, preferred_element_type=jnp.float32
    ).reshape(owned, 2, FF, width)
    rows_grad = jnp.einsum(
        "enf,efd->end", both_grad, in_flat, preferred_element_type=jnp.float32
    ).astype(jnp.bfloat16)
    in_total = lax.psum_scatter(
        in_grad.astype(jnp.bfloat16), "shard", scatter_dimension=2, tiled=True
    ).astype(jnp.float32)
    back = lax.all_to_all(
        rows_grad[None], "expert", split_axis=2, concat_axis=0, tiled=True
    ).reshape(experts * capacity, width)
    norm_two_grad = jnp.sum(back[flat].reshape(rows, top, width).astype(jnp.float32), axis=1)
    select_grad = gates * (gate_grads - jnp.sum(gates * gate_grads, axis=-1, keepdims=True))
    logit_grad = jnp.sum(jnp.where(chosen, select_grad[:, :, None], 0.0), axis=1).astype(
        jnp.bfloat16
    )
    norm_two_grad = norm_two_grad + jnp.dot(
        logit_grad, router_all.T, preferred_element_type=jnp.float32
    )
    router_grad = jnp.dot(norm_two.T, logit_grad, preferred_element_type=jnp.float32)
    gain_two_grad = jnp.sum(norm_two_grad * middle * scale_two, axis=0)
    middle_grad = out_grad + norm_back(middle, scale_two, gain_two, norm_two_grad)
    branch_grad = middle_grad.astype(jnp.bfloat16)
    out_proj_grad = jnp.dot(attended.T, branch_grad, preferred_element_type=jnp.float32)
    attended_grad = jnp.dot(branch_grad, out_all.T, preferred_element_type=jnp.float32).astype(
        jnp.bfloat16
    )
    attended_grad4 = attended_grad.reshape(rows, KVH, repeat, HD)
    recomputed = jnp.exp(score_block() - log_total)
    prob_grad = jnp.einsum(
        "qkrd,tkd->krqt", attended_grad4, value3, preferred_element_type=jnp.float32
    )
    offset = jnp.sum(recomputed * prob_grad, axis=-1, keepdims=True)
    score_grad = (recomputed * (prob_grad - offset)).astype(jnp.bfloat16)
    query_grad = (
        jnp.einsum("krqt,tkd->qkrd", score_grad, key3, preferred_element_type=jnp.float32) * 0.125
    )
    key_grad = (
        jnp.einsum("krqt,qkrd->tkd", score_grad, query4, preferred_element_type=jnp.float32) * 0.125
    )
    value_grad = jnp.einsum(
        "krqt,qkrd->tkd",
        recomputed.astype(jnp.bfloat16),
        attended_grad4,
        preferred_element_type=jnp.float32,
    )
    key_own, value_own = (
        lax.psum_scatter(
            key_grad.reshape(length, kv_dim).astype(jnp.bfloat16),
            "expert",
            scatter_dimension=0,
            tiled=True,
        ).astype(jnp.float32),
        lax.psum_scatter(
            value_grad.reshape(length, kv_dim).astype(jnp.bfloat16),
            "expert",
            scatter_dimension=0,
            tiled=True,
        ).astype(jnp.float32),
    )
    query_raw = rotary(query_grad.reshape(rows, HQ, HD), positions, -1.0).reshape(rows, heads_dim)
    key_raw = rotary(key_own.reshape(rows, KVH, HD), positions, -1.0).reshape(rows, kv_dim)
    proj_grad = jnp.concatenate([query_raw, key_raw, value_own], axis=-1).astype(jnp.bfloat16)
    qkv_grad = jnp.dot(norm_one.T, proj_grad, preferred_element_type=jnp.float32)
    norm_one_grad = jnp.dot(proj_grad, qkv_all.T, preferred_element_type=jnp.float32)
    gain_one_grad = jnp.sum(norm_one_grad * inputs * scale_one, axis=0)
    input_grad = middle_grad + norm_back(inputs, scale_one, gain_one, norm_one_grad)
    gains_grad = jnp.stack([gain_one_grad, gain_two_grad], axis=0)
    dense_shards = (
        lax.psum_scatter(
            qkv_grad.astype(jnp.bfloat16), "shard", scatter_dimension=0, tiled=True
        ).astype(jnp.float32),
        lax.psum_scatter(
            out_proj_grad.astype(jnp.bfloat16), "shard", scatter_dimension=0, tiled=True
        ).astype(jnp.float32),
        lax.psum_scatter(
            router_grad.astype(jnp.bfloat16), "shard", scatter_dimension=0, tiled=True
        ).astype(jnp.float32),
        lax.psum_scatter(
            gains_grad.astype(jnp.bfloat16), "shard", scatter_dimension=1, tiled=True
        ).astype(jnp.float32),
    )
    qkv_total, out_total, router_total, gains_total = (
        lax.psum(dense_shards[0].astype(jnp.bfloat16), "expert").astype(jnp.float32),
        lax.psum(dense_shards[1].astype(jnp.bfloat16), "expert").astype(jnp.float32),
        lax.psum(dense_shards[2].astype(jnp.bfloat16), "expert").astype(jnp.float32),
        lax.psum(dense_shards[3].astype(jnp.bfloat16), "expert").astype(jnp.float32),
    )
    rates = (
        3.0 * D ** (-0.5),
        3.0 * (HQ * HD * 8 // length) ** (-0.5),
        3.0 * (4 * D) ** (-0.5),
        0.6,
        3.0 * D ** (-0.5),
        3.0 * (FF // 16) ** (-0.5),
    )
    decays = (weight_decay, weight_decay, weight_decay, 0.0, weight_decay, weight_decay)
    masters = (qkv_w, out_w, router_w, gains, expert_in, expert_out)
    firsts = (qkv_m, out_m, router_m, gains_m, in_m, down_m)
    seconds = (qkv_v, out_v, router_v, gains_v, in_v, down_v)
    totals = (qkv_total, out_total, router_total, gains_total, in_total, down_total)
    updated = []
    for index in range(6):
        updated.extend(
            adam_step(
                masters[index],
                firsts[index],
                seconds[index],
                totals[index],
                rates[index],
                decays[index],
            )
        )
    return (
        output[None],
        input_grad[None],
        updated[0],
        updated[1],
        updated[2],
        updated[3],
        updated[4],
        updated[5],
        updated[6],
        updated[7],
        updated[8],
        updated[9],
        updated[10],
        updated[11],
        updated[12],
        updated[13],
        updated[14],
        updated[15],
        updated[16],
        updated[17],
    )


def solution(mesh):
    in_specs = (
        P("shard", "expert", None),
        P("shard", "expert", None),
        P("shard", "expert", None),
        P("shard", None),
        P("shard", None),
        P("shard", None),
        P("shard", None),
        P("shard", None),
        P("shard", None),
        P("shard", None),
        P("shard", None),
        P("shard", None),
        P(None, "shard"),
        P(None, "shard"),
        P(None, "shard"),
        P("expert", None, "shard", None),
        P("expert", None, "shard", None),
        P("expert", None, "shard", None),
        P("expert", "shard", None),
        P("expert", "shard", None),
        P("expert", "shard", None),
    )
    out_specs = (
        P("shard", "expert", None),
        P("shard", "expert", None),
        P("shard", None),
        P("shard", None),
        P("shard", None),
        P("shard", None),
        P("shard", None),
        P("shard", None),
        P("shard", None),
        P("shard", None),
        P("shard", None),
        P(None, "shard"),
        P(None, "shard"),
        P(None, "shard"),
        P("expert", None, "shard", None),
        P("expert", None, "shard", None),
        P("expert", None, "shard", None),
        P("expert", "shard", None),
        P("expert", "shard", None),
        P("expert", "shard", None),
    )
    return jax.shard_map(body, mesh=mesh, in_specs=in_specs, out_specs=out_specs, check_vma=False)
```

profile of v0, /device:TPU:8, one launch (start us, length us, event | category | flops | bytes accessed | tf_op | source)
XLA Modules:
  0.0 1221.1 jit_solution(18065714152636872095)
XLA Ops:
  10.1 17.9 %all_gather.24 = bf16[2,1024]{1,0:T(2,128)(2,1)S(1)} all-gather(bf16[2,128]{1,0:T(2,128)(2,1)S(1)} %convert_element_type.193), channel_id=1, replica_groups=mesh['expert'=4,'shard'=8] {'shard'}, dimensions={1}, use_global_device_ids=true | all-gather | bytes 4608 | tf_op jit(solution)/shard_map/all_gather | solution.py:103
  29.8 54.9 %all-gather.7.cloned.1.call-done = bf16[1024,2048]{1,0:T(8,128)(2,1)} async-done(((bf16[128,2048]{1,0:T(8,128)(2,1)}), bf16[1024,2048]{1,0:T(8,128)(2,1)}) %all-gather.7.cloned.1.call-update) | async-done | bytes 4194320 | tf_op jit(solution)/shard_map/all_gather | solution.py:100
  102.6 8.2 scatter_custom_fusion
  113.3 12.0 all-gather.11.cloned.1.call-done
  125.3 8.6 fusion.77
  133.8 8.3 exponential_reduce_fusion
  142.2 8.5 fusion.17
  150.8 26.4 %all-gather.13.cloned.1.call-done = bf16[1024,1024]{1,0:T(8,128)(2,1)} async-done(((bf16[128,1024]{1,0:T(8,128)(2,1)}), bf16[1024,1024]{1,0:T(8,128)(2,1)}) %all-gather.13.cloned.1.call-update) | async-done | bytes 2097168 | tf_op jit(solution)/shard_map/all_gather | solution.py:101
  194.5 25.1 %all_gather.29 = bf16[1024,16]{0,1:T(8,128)(2,1)S(1)} all-gather(bf16[128,16]{0,1:T(8,128)(2,1)S(1)} %convert_element_type.204), channel_id=1, replica_groups=mesh['expert'=4,'shard'=8] {'shard'}, dimensions={0}, use_global_device_ids=true | all-gather | bytes 36864 | tf_op jit(solution)/shard_map/all_gather | solution.py:102
  223.4 13.7 %gather_fusion.2 = bf16[2176,1024]{1,0:T(8,128)(2,1)} fusion(bf16[2049,1024]{1,0:T(8,128)(2,1)} %concatenate.40, s32[3072]{0:T(1024)S(1)} %get-tuple-element.80), kind=kCustom, calls=%fused_computation.2 | custom fusion | bytes 8921600 | tf_op jit(solution)/shard_map/gather | solution.py:178
  254.7 46.0 %all-to-all-done.2 = bf16[4,4,136,1024]{3,2,1,0:T(8,128)(2,1)} async-done(((bf16[4,4,136,1024]{3,2,1,0:T(8,128)(2,1)}), bf16[4,4,136,1024]{3,2,1,0:T(8,128)(2,1)}, u32[]{:S(2)}, u32[]{:S(2)}) %all-to-all-start.2) | async-done | bytes 4456480 | tf_op jit(solution)/shard_map/all_to_all | solution.py:179
  305.6 13.0 %fusion.79 = f32[4,544,1024]{2,1,0:T(8,128)} fusion(bf16[4,544,1024]{2,1,0:T(8,128)(2,1)} %bitcast.177, bf16[4,1024,1024]{2,1,0:T(8,128)(2,1)} %bitcast.217), kind=kOutput, calls=%fused_computation.175 | convolution fusion | flops 4563402752 | bytes 21757952 | tf_op jit(solution)/shard_map/end,efd->enf/dot_general | solution.py:160
  318.7 58.7 %all-gather.17.cloned.1.call-done = bf16[4,512,1024]{2,1,0:T(8,128)(2,1)} async-done(((bf16[4,64,1024]{2,1,0:T(8,128)(2,1)}), bf16[4,512,1024]{2,1,0:T(8,128)(2,1)}) %all-gather.17.cloned.1.call-update) | async-done | bytes 4194320 | tf_op jit(solution)/shard_map/all_gather | solution.py:107
  377.4 11.6 multiply_convert_fusion.1
  389.0 10.4 convert_bitcast_fusion
  420.7 40.1 %all-to-all-done.3 = bf16[1,4,544,1024]{3,1,0,2:T(4,128)(2,1)} async-done(((bf16[1,4,544,1024]{3,1,0,2:T(4,128)(2,1)}), bf16[1,4,544,1024]{3,1,0,2:T(4,128)(2,1)}, u32[]{:S(2)}, u32[]{:S(2)}) %all-to-all-start.3) | async-done | bytes 4456480 | tf_op jit(solution)/shard_map/all_to_all | solution.py:202
  471.6 14.0 %gather_fusion.3 = bf16[2048,1024]{1,0:T(8,128)(2,1)} fusion(bf16[2176,1024]{1,0:T(8,128)(2,1)} %bitcast.164, s32[2048]{0:T(1024)S(1)} %broadcast_clamp_fusion), kind=kCustom, calls=%fused_computation.3 | custom fusion | bytes 8396800 | tf_op jit(solution)/shard_map/gather | solution.py:205
  492.1 24.7 %all-to-all-done.1 = bf16[1,4,544,1024]{3,1,0,2:T(4,128)(2,1)} async-done(((bf16[1,4,544,1024]{3,1,0,2:T(4,128)(2,1)}), bf16[1,4,544,1024]{3,1,0,2:T(4,128)(2,1)}, u32[]{:S(2)}, u32[]{:S(2)}) %all-to-all-start.1) | async-done | bytes 4456480 | tf_op jit(solution)/shard_map/all_to_all | solution.py:167
  522.7 13.8 %gather_fusion.1 = bf16[2048,1024]{1,0:T(8,128)(2,1)} fusion(bf16[2176,1024]{1,0:T(8,128)(2,1)} %bitcast.163, s32[2048]{0:T(1024)S(1)} %broadcast_clamp_fusion), kind=kCustom, calls=%fused_computation.1 | custom fusion | bytes 8396800 | tf_op jit(solution)/shard_map/gather | solution.py:170
  551.1 16.3 %fusion = (f32[8,2,256]{2,1,0:T(2,128)}, f32[8,1024,256,2]{2,1,3,0:T(8,128)}) fusion(f32[8,2,256,1024]{2,3,1,0:T(8,128)} %get-tuple-element.73, f32[8,2,256]{2,1,0:T(2,128)} %bitcast.195, bf16[1024,8,64,1]{0,2,3,1:T(8,128)(2,1)} %bitcast.168, bf16[256,8,2,64]{0,3,2,1:T(8,128)(2,1)} %bitcast.173), kind=kOutput, calls=%fused_computation.7 | convolution fusion | flops 549449728 | bytes 35160064 | tf_op jit(solution)/shard_map/qkrd,tkd->krqt/dot_general | solution.py:223
  567.5 10.1 fusion.2
  584.8 9.8 bitcast_convert_fusion
  608.8 27.1 %reduce-scatter.15.cloned.1.call-done = bf16[256,512]{0,1:T(8,128)(2,1)} async-done(((bf16[1024,512]{0,1:T(8,128)(2,1)}), bf16[256,512]{0,1:T(8,128)(2,1)}) %reduce-scatter.15.cloned.1.call-update) | async-done | bytes 262160 | tf_op jit(solution)/shard_map/reduce_scatter | solution.py:247
  647.2 8.4 convolution_convert_fusion.2
  655.7 51.3 %reduce-scatter.19.cloned.1.call-done = bf16[128,1024]{1,0:T(8,128)(2,1)} async-done(((bf16[1024,1024]{1,0:T(8,128)(2,1)}), bf16[128,1024]{1,0:T(8,128)(2,1)}) %reduce-scatter.19.cloned.1.call-update) | async-done | bytes 262160 | tf_op jit(solution)/shard_map/reduce_scatter | solution.py:266
  707.0 91.3 %reduce-scatter.17.cloned.1.call-done = bf16[128,2048]{1,0:T(8,128)(2,1)} async-done(((bf16[1024,2048]{1,0:T(8,128)(2,1)}), bf16[128,2048]{1,0:T(8,128)(2,1)}) %reduce-scatter.17.cloned.1.call-update) | async-done | bytes 524304 | tf_op jit(solution)/shard_map/reduce_scatter | solution.py:263
  798.4 12.1 convolution_convert_fusion
  810.6 52.8 %reduce-scatter.25.cloned.1.call-done = bf16[128,16]{1,0:T(8,128)(2,1)} async-done(((bf16[1024,16]{1,0:T(8,128)(2,1)}), bf16[128,16]{1,0:T(8,128)(2,1)}) %reduce-scatter.25.cloned.1.call-update) | async-done | bytes 4112
  866.7 61.1 %reduce-scatter.27.cloned.1.call-done = bf16[128,2]{1,0:T(8,128)(2,1)} async-done(((bf16[1024,2]{1,0:T(8,128)(2,1)}), bf16[128,2]{1,0:T(8,128)(2,1)}) %reduce-scatter.27.cloned.1.call-update) | async-done | bytes 528
  935.9 83.7 %reduce-scatter.23.cloned.1.call-done = bf16[4,64,1024]{2,1,0:T(8,128)(2,1)} async-done(((bf16[4,512,1024]{2,1,0:T(8,128)(2,1)}), bf16[4,64,1024]{2,1,0:T(8,128)(2,1)}) %reduce-scatter.23.cloned.1.call-update) | async-done | bytes 524304 | tf_op jit(solution)/shard_map/reduce_scatter | solution.py:183
  1023.6 32.6 %all-reduce.6.cloned.1.call-done = (bf16[128,2048]{1,0:T(8,128)(2,1)}, bf16[128,1024]{1,0:T(8,128)(2,1)}) async-done(((bf16[128,2048]{1,0:T(8,128)(2,1)}, bf16[128,1024]{1,0:T(8,128)(2,1)}), (bf16[128,2048]{1,0:T(8,128)(2,1)}, bf16[128,1024]{1,0:T(8,128)(2,1)})) %all-reduce.6.cloned.1.call-update) | async-done | bytes 786448 | tf_op jit(solution)/shard_map/psum | solution.py:277
  1063.1 144.4 %reduce-scatter.21.cloned.1.call-done = bf16[4,2,64,1024]{3,2,1,0:T(8,128)(2,1)} async-done(((bf16[4,2,512,1024]{3,2,1,0:T(8,128)(2,1)}), bf16[4,2,64,1024]{3,2,1,0:T(8,128)(2,1)}) %reduce-scatter.21.cloned.1.call-update) | async-done | bytes 1048592 | tf_op jit(solution)/shard_map/reduce_scatter | solution.py:199
  (237 shorter events, 188.7 us)
Async XLA Ops:
  7.2 77.5 %all-gather.7.cloned.1.call-start = ((), (), s32[]{:S(2)}) async-start(), calls=%async_computation.12 | async-start | bytes 4718592 | tf_op jit(solution)/shard_map/all_gather | solution.py:100
  9.3 102.3 %all-gather.9.cloned.1.call-start = ((), (), s32[]{:S(2)}) async-start(), calls=%async_computation.13 | async-start | bytes 1310720 | tf_op jit(solution)/shard_map/all_gather | solution.py:124
  29.8 54.9 %copy-start.35 = (f32[256]{0:T(256)}, f32[256]{0:T(256)S(1)}, u32[]{:S(2)}) copy-start(f32[256]{0:T(256)S(1)} %get-tuple-element.69) | copy-start | bytes 3076
  29.8 54.9 %copy-start.28 = (f32[1,1024]{1,0:T(1,128)}, f32[1,1024]{1,0:T(1,128)S(1)}, u32[]{:S(2)}) copy-start(f32[1,1024]{1,0:T(1,128)S(1)} %get-tuple-element.64) | copy-start | bytes 12292
  90.5 34.8 %all-gather.11.cloned.1.call-start = ((), (), s32[]{:S(2)}) async-start(), calls=%async_computation.14 | async-start | bytes 1310720 | tf_op jit(solution)/shard_map/all_gather | solution.py:123
  93.5 83.6 %all-gather.13.cloned.1.call-start = ((), (), s32[]{:S(2)}) async-start(), calls=%async_computation.15 | async-start | bytes 2359296 | tf_op jit(solution)/shard_map/all_gather | solution.py:101
  95.4 210.3 %all-gather.15.cloned.1.call-start = ((), (), s32[]{:S(2)}) async-start(), calls=%async_computation.16 | async-start | bytes 9437184 | tf_op jit(solution)/shard_map/all_gather | solution.py:106
  180.1 362.8 %copy-start.30 = (f32[256]{0:T(256)}, f32[256]{0:T(256)S(1)}, u32[]{:S(2)}) copy-start(f32[256]{0:T(256)S(1)} %get-tuple-element.71) | copy-start | bytes 3076
  188.5 56.1 %all-to-all-start = ((bf16[4,4,136,1024]{3,2,1,0:T(8,128)(2,1)}), bf16[4,4,136,1024]{3,2,1,0:T(8,128)(2,1)}, u32[]{:S(2)}, u32[]{:S(2)}) async-start(bf16[4,4,136,1024]{3,2,1,0:T(8,128)(2,1)} %bitcast.165), calls=%async_computation | async-start | bytes 8912896 | tf_op jit(solution)/shard_map/all_to_all | solution.py:159
  193.5 183.8 %all-gather.17.cloned.1.call-start = ((), (), s32[]{:S(2)}) async-start(), calls=%async_computation.17 | async-start | bytes 4718592 | tf_op jit(solution)/shard_map/all_gather | solution.py:107
  244.5 56.1 %all-to-all-start.2 = ((bf16[4,4,136,1024]{3,2,1,0:T(8,128)(2,1)}), bf16[4,4,136,1024]{3,2,1,0:T(8,128)(2,1)}, u32[]{:S(2)}, u32[]{:S(2)}) async-start(bf16[4,4,136,1024]{3,2,1,0:T(8,128)(2,1)} %bitcast.166), calls=%async_computation.2 | async-start | bytes 8912896 | tf_op jit(solution)/shard_map/all_to_all | solution.py:179
  404.9 55.9 %all-to-all-start.3 = ((bf16[1,4,544,1024]{3,1,0,2:T(4,128)(2,1)}), bf16[1,4,544,1024]{3,1,0,2:T(4,128)(2,1)}, u32[]{:S(2)}, u32[]{:S(2)}) async-start(bf16[1,4,544,1024]{3,1,0,2:T(4,128)(2,1)} %copy.130), calls=%async_computation.3 | async-start | bytes 8912896 | tf_op jit(solution)/shard_map/all_to_all | solution.py:202
  460.8 55.9 %all-to-all-start.1 = ((bf16[1,4,544,1024]{3,1,0,2:T(4,128)(2,1)}), bf16[1,4,544,1024]{3,1,0,2:T(4,128)(2,1)}, u32[]{:S(2)}, u32[]{:S(2)}) async-start(bf16[1,4,544,1024]{3,1,0,2:T(4,128)(2,1)} %copy.126), calls=%async_computation.1 | async-start | bytes 8912896 | tf_op jit(solution)/shard_map/all_to_all | solution.py:167
  465.7 142.0 %reduce-scatter.13.cloned.1.call-start = ((), (), s32[]{:S(2)}) async-start(), calls=%async_computation.18 | async-start | bytes 1310720 | tf_op jit(solution)/shard_map/reduce_scatter | solution.py:241
  584.7 51.2 %reduce-scatter.15.cloned.1.call-start = ((), (), s32[]{:S(2)}) async-start(), calls=%async_computation.19 | async-start | bytes 1310720 | tf_op jit(solution)/shard_map/reduce_scatter | solution.py:247
  594.6 112.4 %reduce-scatter.19.cloned.1.call-start = ((), (), s32[]{:S(2)}) async-start(), calls=%async_computation.21 | async-start | bytes 2359296 | tf_op jit(solution)/shard_map/reduce_scatter | solution.py:266
  596.8 201.6 %reduce-scatter.17.cloned.1.call-start = ((), (), s32[]{:S(2)}) async-start(), calls=%async_computation.20 | async-start | bytes 4718592 | tf_op jit(solution)/shard_map/reduce_scatter | solution.py:263
  640.5 222.9 %reduce-scatter.25.cloned.1.call-start = ((), (), s32[]{:S(2)}) async-start(), calls=%async_computation.24 | async-start | bytes 294912
  641.6 286.1 %reduce-scatter.27.cloned.1.call-start = ((), (), s32[]{:S(2)}) async-start(), calls=%async_computation.25 | async-start | bytes 294912
  647.2 372.5 %reduce-scatter.23.cloned.1.call-start = ((), (), s32[]{:S(2)}) async-start(), calls=%async_computation.23 | async-start | bytes 4718592 | tf_op jit(solution)/shard_map/reduce_scatter | solution.py:183
  655.6 400.6 %all-reduce.6.cloned.1.call-start = ((), (), s32[]{:S(2)}) async-start(), calls=%async_computation.26 | async-start | bytes 1572864 | tf_op jit(solution)/shard_map/psum | solution.py:277
  798.4 409.2 %reduce-scatter.21.cloned.1.call-start = ((), (), s32[]{:S(2)}) async-start(), calls=%async_computation.22 | async-start | bytes 9437184 | tf_op jit(solution)/shard_map/reduce_scatter | solution.py:199
  810.5 53.7 %copy-start.34 = (f32[256]{0:T(256)S(1)}, f32[256]{0:T(256)}, u32[]{:S(2)}) copy-start(f32[256]{0:T(256)} %get-tuple-element.68) | copy-start | bytes 3076
  810.5 124.2 %copy-start.37 = (f32[2,128]{1,0:T(2,128)S(1)}, f32[2,128]{1,0:T(2,128)}, u32[]{:S(2)}) copy-start(f32[2,128]{1,0:T(2,128)} %param.33) | copy-start | bytes 3076
  810.5 124.2 %copy-start.38 = (f32[2,128]{1,0:T(2,128)S(1)}, f32[2,128]{1,0:T(2,128)}, u32[]{:S(2)}) copy-start(f32[2,128]{1,0:T(2,128)} %param.35) | copy-start | bytes 3076
  810.5 124.2 %copy-start.39 = (f32[2,128]{1,0:T(2,128)S(1)}, f32[2,128]{1,0:T(2,128)}, u32[]{:S(2)}) copy-start(f32[2,128]{1,0:T(2,128)} %param.34) | copy-start | bytes 3076
  810.5 124.8 %copy-start.27 = (f32[128,16]{0,1:T(8,128)S(1)}, f32[128,16]{0,1:T(8,128)}, u32[]{:S(2)}) copy-start(f32[128,16]{0,1:T(8,128)} %param.30) | copy-start | bytes 24580
  810.5 124.8 %copy-start.32 = (f32[128,16]{0,1:T(8,128)S(1)}, f32[128,16]{0,1:T(8,128)}, u32[]{:S(2)}) copy-start(f32[128,16]{0,1:T(8,128)} %param.32) | copy-start | bytes 24580
  810.5 124.7 %copy-start.33 = (f32[128,16]{0,1:T(8,128)S(1)}, f32[128,16]{0,1:T(8,128)}, u32[]{:S(2)}) copy-start(f32[128,16]{0,1:T(8,128)} %param.31) | copy-start | bytes 24580
  810.5 209.1 %copy-start.13 = (f32[4,64,1024]{2,1,0:T(8,128)S(1)}, f32[4,64,1024]{2,1,0:T(8,128)}, u32[]{:S(2)}) copy-start(f32[4,64,1024]{2,1,0:T(8,128)} %param.39) | copy-start | bytes 3145732
  935.9 123.3 %copy-start.14 = (f32[128,2048]{1,0:T(8,128)S(1)}, f32[128,2048]{1,0:T(8,128)}, u32[]{:S(2)}) copy-start(f32[128,2048]{1,0:T(8,128)} %param.24) | copy-start | bytes 3145732
  1056.2 151.3 %copy-start.4 = (f32[4,2,64,1024]{3,2,1,0:T(8,128)S(1)}, f32[4,2,64,1024]{3,2,1,0:T(8,128)}, u32[]{:S(2)}) copy-start(f32[4,2,64,1024]{3,2,1,0:T(8,128)} %param.36) | copy-start | bytes 6291460
  (35 other events, 540.2 us)
Sparse Core Ops, SparseCore 0:
  10.7 73.9 all-gather.6
  90.6 15.6 all-gather.8
  108.4 16.8 all-gather.10
  127.8 49.2 all-gather.12
  179.8 122.1 all-gather.14
  304.6 72.7 all-gather.16
  584.8 22.8 reduce-scatter.12
  611.0 24.8 reduce-scatter.14
  640.1 66.9 reduce-scatter.18
  710.5 87.7 reduce-scatter.16
  802.6 60.6 reduce-scatter.24
  867.5 60.2 reduce-scatter.26
  931.8 87.7 reduce-scatter.22
  1022.0 34.1 all-reduce.5
  1059.7 147.7 reduce-scatter.20
where the time goes:
time: 1230 us; the launch traced here: 1220 us
  waiting for transfers between devices  820 us (67%)
  matrix products  138 us (11%)
  local copies, waits for them, and re-layouts  104 us (8%)
  other arithmetic  72.9 us (6%)
  blocking collectives  49.1 us (4%)
  starting transfers between devices  20.8 us (2%)
  between operations  15.4 us (1%)
    reduce_scatter x1, waiting for transfers between devices, body(): lax.psum_scatter(in_grad.astype(jnp.bfloat16), 'shard', scatter_dimension...  144 us
    unnamed x17, waiting for transfers between devices  114 us
    reduce_scatter x1, waiting for transfers between devices, body(): lax.psum_scatter(qkv_grad.astype(jnp.bfloat16), 'shard', scatter_dimensio...  91.3 us
    reduce_scatter x1, waiting for transfers between devices, body(): lax.psum_scatter(down_grad.astype(jnp.bfloat16), 'shard', scatter_dimensi...  83.7 us
    all_gather x1, waiting for transfers between devices, body(): lax.all_gather(expert_out.astype(jnp.bfloat16), 'shard', axis=1, tiled=True)  58.7 us
    all_gather x1, waiting for transfers between devices, body(): lax.all_gather(qkv_w.astype(jnp.bfloat16), 'shard', axis=0, tiled=True)  54.9 us
    reduce_scatter x1, waiting for transfers between devices, body(): lax.psum_scatter(out_proj_grad.astype(jnp.bfloat16), 'shard', scatter_dim...  51.3 us
    all_to_all x1, waiting for transfers between devices, body(): lax.all_to_all(grad_sending, 'expert', split_axis=0, concat_axis=2, tiled...  46 us
  transfers between devices with their start and end apart: 19, of which 17 were waited for; matrix products, arithmetic and copies ran while one was open for 17% of the time, Pallas kernels for 0%

commit v1 on v0

v1 whole, which is shorter than its diff:
```python
import math

import jax
import jax.numpy as jnp
from jax import lax
from jax.sharding import PartitionSpec as P

D = 1024
HQ = 16
KVH = 8
HD = 64
FF = 512
STEP = 10

EXPERT = ("x", "core")
SHARD = ("z", "y")
ALL = ("z", "y", "x", "core")
GROUP = ("x", "core", "y")


beta_one = 0.9
beta_two = 0.95
adam_eps = 1e-08
weight_decay = 0.1
norm_eps = 1e-05
rope_base = 10000.0
masked_score = -1e30


def rms_scale(values):
    return lax.rsqrt(jnp.mean(values * values, axis=-1, keepdims=True) + norm_eps)


def norm_back(values, scale, gain, grad):
    weighted = gain * grad
    inner = jnp.mean(values * weighted, axis=-1, keepdims=True)
    return scale * weighted - values * (scale * scale * scale) * inner


def rotary(values, positions, sign):
    half = values.shape[-1] // 2
    freqs = rope_base ** (-jnp.arange(half, dtype=jnp.float32) / half)
    angles = positions.astype(jnp.float32)[:, None] * freqs[None, :]
    cosine = jnp.cos(angles)[:, None, :]
    sine = sign * jnp.sin(angles)[:, None, :]
    first = values[..., :half]
    second = values[..., half:]
    return jnp.concatenate(
        [first * cosine - second * sine, second * cosine + first * sine], axis=-1
    )


def adam_step(weight, first, second, grad, rate, decay):
    new_first = beta_one * first + (1.0 - beta_one) * grad
    new_second = beta_two * second + (1.0 - beta_two) * grad * grad
    fix_one = 1.0 - beta_one**STEP
    fix_two = 1.0 - beta_two**STEP
    update = new_first / fix_one / (jnp.sqrt(new_second / fix_two) + adam_eps)
    return (new_first, new_second, weight - rate * (update + decay * weight))


def body(
    tokens,
    cotangent,
    routes,
    qkv_w,
    qkv_m,
    qkv_v,
    out_w,
    out_m,
    out_v,
    router_w,
    router_m,
    router_v,
    gains,
    gains_m,
    gains_v,
    expert_in,
    in_m,
    in_v,
    expert_out,
    down_m,
    down_v,
):
    rows = tokens.shape[1]
    width = tokens.shape[2]
    spread = lax.axis_size(EXPERT)
    length = rows * spread
    experts = router_w.shape[1]
    owned = expert_in.shape[0]
    heads_dim = HQ * HD
    kv_dim = KVH * HD
    repeat = HQ // KVH
    low = jnp.bfloat16
    high = jnp.float32
    own = lax.axis_index(EXPERT)
    part = qkv_w.shape[0] // spread

    def own_part(weight):
        return lax.dynamic_slice_in_dim(weight, own * part, part, axis=0).astype(low)

    qkv_all = lax.all_gather(own_part(qkv_w), ALL, axis=0, tiled=True)
    gains_all = lax.all_gather(gains.astype(low), SHARD, axis=1, tiled=True).astype(high)
    out_all = lax.all_gather(own_part(out_w), ALL, axis=0, tiled=True)
    router_all = lax.all_gather(own_part(router_w), ALL, axis=0, tiled=True)
    gate_w = lax.all_gather(expert_in[:, 0].astype(low), "z", axis=1, tiled=True)
    up_w = lax.all_gather(expert_in[:, 1].astype(low), "z", axis=1, tiled=True)
    down_w = lax.all_gather(expert_out.astype(low), "z", axis=1, tiled=True)
    hidden = gate_w.shape[1]
    gate_w = gate_w.reshape(owned * hidden, width)
    up_w = up_w.reshape(owned * hidden, width)
    down_w = down_w.reshape(owned * hidden, width)
    routes_all = lax.all_gather(routes[0], GROUP, axis=0, tiled=True)
    grad_all = lax.all_gather(cotangent[0], GROUP, axis=0, tiled=True)
    chosen = jnp.any(
        routes_all[:, :, None] == jnp.arange(experts, dtype=jnp.int32)[None, None, :], axis=1
    )

    gain_one = gains_all[0]
    gain_two = gains_all[1]
    inputs = tokens[0].astype(high)
    scale_one = rms_scale(inputs)
    norm_one = (inputs * scale_one * gain_one).astype(low)
    proj = jnp.dot(norm_one, qkv_all, preferred_element_type=high)
    positions = own * rows + jnp.arange(rows, dtype=jnp.int32)
    query = rotary(proj[:, :heads_dim].reshape(rows, HQ, HD), positions, 1.0).astype(low)
    key = rotary(
        proj[:, heads_dim : heads_dim + kv_dim].reshape(rows, KVH, HD), positions, 1.0
    ).astype(low)
    value = proj[:, heads_dim + kv_dim :].astype(low)
    both_all = lax.all_gather(
        jnp.concatenate([key.reshape(rows, kv_dim), value], axis=1), EXPERT, axis=0, tiled=True
    )
    query4 = query.reshape(rows, KVH, repeat, HD)
    key3 = both_all[:, :kv_dim].reshape(length, KVH, HD)
    value3 = both_all[:, kv_dim:].reshape(length, KVH, HD)
    causal = jnp.arange(length, dtype=jnp.int32)[None, :] <= positions[:, None]
    raw = jnp.einsum("qkrd,tkd->krqt", query4, key3, preferred_element_type=high) * 0.125
    masked = jnp.where(causal, raw, masked_score)
    probs = jax.nn.softmax(masked, axis=-1).astype(low)
    attended = jnp.einsum("krqt,tkd->qkrd", probs, value3, preferred_element_type=high)
    attended = attended.reshape(rows, heads_dim).astype(low)
    middle = inputs + jnp.dot(attended, out_all, preferred_element_type=high)
    scale_two = rms_scale(middle)
    norm_two = (middle * scale_two * gain_two).astype(low)

    norm_all = lax.all_gather(norm_two, GROUP, axis=0, tiled=True)
    logits = jnp.dot(norm_all, router_all, preferred_element_type=high)
    gates = jax.nn.softmax(jnp.where(chosen, logits, masked_score), axis=-1)
    own_gates = lax.dynamic_slice_in_dim(gates, own * owned, owned, axis=1)
    count = norm_all.shape[0]

    def per_expert(values):
        return values.reshape(count, owned, hidden)

    def dot_rows(first, second):
        return lax.dot_general(
            first, second, (((1,), (1,)), ((), ())), preferred_element_type=high
        )

    def dot_tokens(first, second):
        return lax.dot_general(
            first, second, (((0,), (0,)), ((), ())), preferred_element_type=high
        )

    gate_part = dot_rows(norm_all, gate_w)
    up_part = dot_rows(norm_all, up_w)
    sigmoid = jax.nn.sigmoid(gate_part)
    active = gate_part * sigmoid * up_part
    wide_gates = jnp.repeat(own_gates, hidden, axis=1)
    weighted = (active * wide_gates).astype(low)
    results = jnp.dot(weighted, down_w, preferred_element_type=high)
    mixed = lax.psum_scatter(results.astype(low), GROUP, scatter_dimension=0, tiled=True)
    output = (middle + mixed.astype(high)).astype(low)
    down_grad = dot_tokens(weighted, grad_all)
    down_total = lax.psum_scatter(
        down_grad.astype(low).reshape(owned, hidden, width), "z", scatter_dimension=1, tiled=True
    )
    plain_grad = dot_rows(grad_all, down_w)
    gate_grads = jnp.sum(per_expert(plain_grad * active), axis=2) * own_gates
    active_grad = plain_grad * wide_gates
    gate_grad = (active_grad * up_part * sigmoid * (1.0 + gate_part * (1.0 - sigmoid))).astype(low)
    up_grad = (active_grad * gate_part * sigmoid).astype(low)
    logit_grad = lax.dynamic_update_slice_in_dim(
        jnp.zeros((count, experts), high), gate_grads, own * owned, axis=1
    ) - gates * jnp.sum(gate_grads, axis=1, keepdims=True)
    logit_grad = logit_grad.astype(low)
    rows_grad = (
        jnp.dot(gate_grad, gate_w, preferred_element_type=high)
        + jnp.dot(up_grad, up_w, preferred_element_type=high)
        + dot_rows(logit_grad, router_all)
    )
    norm_two_grad = lax.psum_scatter(
        rows_grad.astype(low), GROUP, scatter_dimension=0, tiled=True
    ).astype(high)
    gate_total = lax.psum_scatter(
        dot_tokens(gate_grad, norm_all).astype(low).reshape(owned, hidden, width),
        "z",
        scatter_dimension=1,
        tiled=True,
    )
    up_total = lax.psum_scatter(
        dot_tokens(up_grad, norm_all).astype(low).reshape(owned, hidden, width),
        "z",
        scatter_dimension=1,
        tiled=True,
    )
    router_grad = dot_tokens(norm_all, logit_grad)

    out_grad = cotangent[0].astype(high)
    gain_two_grad = jnp.sum(norm_two_grad * middle * scale_two, axis=0)
    middle_grad = out_grad + norm_back(middle, scale_two, gain_two, norm_two_grad)
    branch_grad = middle_grad.astype(low)
    out_proj_grad = dot_tokens(attended, branch_grad)
    attended_grad = dot_rows(branch_grad, out_all).astype(low)
    attended_grad4 = attended_grad.reshape(rows, KVH, repeat, HD)
    probs_high = probs.astype(high)
    prob_grad = jnp.einsum("qkrd,tkd->krqt", attended_grad4, value3, preferred_element_type=high)
    offset = jnp.sum(probs_high * prob_grad, axis=-1, keepdims=True)
    score_grad = (probs_high * (prob_grad - offset)).astype(low)
    query_grad = (
        jnp.einsum("krqt,tkd->qkrd", score_grad, key3, preferred_element_type=high) * 0.125
    )
    key_grad = (
        jnp.einsum("krqt,qkrd->tkd", score_grad, query4, preferred_element_type=high) * 0.125
    )
    value_grad = jnp.einsum("krqt,qkrd->tkd", probs, attended_grad4, preferred_element_type=high)
    both_grad = jnp.concatenate(
        [key_grad.reshape(length, kv_dim), value_grad.reshape(length, kv_dim)], axis=1
    ).astype(low)
    both_own = lax.psum_scatter(both_grad, EXPERT, scatter_dimension=0, tiled=True)
    query_raw = rotary(query_grad.reshape(rows, HQ, HD), positions, -1.0).reshape(rows, heads_dim)
    key_raw = rotary(
        both_own[:, :kv_dim].astype(high).reshape(rows, KVH, HD), positions, -1.0
    ).reshape(rows, kv_dim)
    proj_grad = jnp.concatenate(
        [query_raw.astype(low), key_raw.astype(low), both_own[:, kv_dim:]], axis=-1
    )
    qkv_grad = dot_tokens(norm_one, proj_grad)
    norm_one_grad = dot_rows(proj_grad, qkv_all)
    gain_one_grad = jnp.sum(norm_one_grad * inputs * scale_one, axis=0)
    input_grad = middle_grad + norm_back(inputs, scale_one, gain_one, norm_one_grad)

    def total_part(grad):
        piece = lax.psum_scatter(grad.astype(low), ALL, scatter_dimension=0, tiled=True)
        return lax.all_gather(piece, EXPERT, axis=0, tiled=True)

    out_total = total_part(out_proj_grad)
    router_total = total_part(router_grad)
    qkv_total = total_part(qkv_grad)
    gains_grad = jnp.stack([gain_one_grad, gain_two_grad], axis=0)
    gains_total = lax.psum(
        lax.psum_scatter(gains_grad, SHARD, scatter_dimension=1, tiled=True), EXPERT
    )
    in_total = jnp.stack([gate_total, up_total], axis=1)
    rates = (
        3.0 * D ** (-0.5),
        3.0 * (HQ * HD * 8 // length) ** (-0.5),
        3.0 * (4 * D) ** (-0.5),
        0.6,
        3.0 * D ** (-0.5),
        3.0 * (FF // 16) ** (-0.5),
    )
    decays = (weight_decay, weight_decay, weight_decay, 0.0, weight_decay, weight_decay)
    masters = (qkv_w, out_w, router_w, gains, expert_in, expert_out)
    firsts = (qkv_m, out_m, router_m, gains_m, in_m, down_m)
    seconds = (qkv_v, out_v, router_v, gains_v, in_v, down_v)
    totals = (qkv_total, out_total, router_total, gains_total, in_total, down_total)
    updated = []
    for index in range(6):
        updated.extend(
            adam_step(
                masters[index],
                firsts[index],
                seconds[index],
                totals[index].astype(high),
                rates[index],
                decays[index],
            )
        )
    return (output[None], input_grad[None], *updated)


def solution(mesh):
    spread = mesh.shape["expert"]
    shards = mesh.shape["shard"]
    short = math.isqrt(shards // 2)
    grid = jax.sharding.Mesh(
        mesh.devices.reshape(spread // 2, 2, shards // short, short), ("x", "core", "z", "y")
    )
    in_specs = (
        P(SHARD, EXPERT, None),
        P(SHARD, EXPERT, None),
        P(SHARD, EXPERT, None),
        P(SHARD, None),
        P(SHARD, None),
        P(SHARD, None),
        P(SHARD, None),
        P(SHARD, None),
        P(SHARD, None),
        P(SHARD, None),
        P(SHARD, None),
        P(SHARD, None),
        P(None, SHARD),
        P(None, SHARD),
        P(None, SHARD),
        P(EXPERT, None, SHARD, None),
        P(EXPERT, None, SHARD, None),
        P(EXPERT, None, SHARD, None),
        P(EXPERT, SHARD, None),
        P(EXPERT, SHARD, None),
        P(EXPERT, SHARD, None),
    )
    out_specs = (
        P(SHARD, EXPERT, None),
        P(SHARD, EXPERT, None),
        P(SHARD, None),
        P(SHARD, None),
        P(SHARD, None),
        P(SHARD, None),
        P(SHARD, None),
        P(SHARD, None),
        P(SHARD, None),
        P(SHARD, None),
        P(SHARD, None),
        P(None, SHARD),
        P(None, SHARD),
        P(None, SHARD),
        P(EXPERT, None, SHARD, None),
        P(EXPERT, None, SHARD, None),
        P(EXPERT, None, SHARD, None),
        P(EXPERT, SHARD, None),
        P(EXPERT, SHARD, None),
        P(EXPERT, SHARD, None),
    )
    return jax.shard_map(body, mesh=grid, in_specs=in_specs, out_specs=out_specs, check_vma=False)
```

time: 1230 us -> 1230 us (level)
  the two profiles are of different devices: /device:TPU:8 before, /device:TPU:0 now
where the time goes in v1:
time: 1230 us; the launch traced here: 1220 us
  waiting for transfers between devices  875 us (71%)
  matrix products  147 us (12%)
  blocking collectives  102 us (8%)
  other arithmetic  64.6 us (5%)
  local copies, waits for them, and re-layouts  19.9 us (2%)
  between operations  15.5 us (1%)
    reduce_scatter x2, waiting for transfers between devices, total_part(): lax.psum_scatter(grad.astype(low), ALL, scatter_dimension=0, tiled=True)  267 us
    unnamed x20, waiting for transfers between devices  169 us
    reduce_scatter x1, waiting for transfers between devices, body(): lax.psum_scatter(results.astype(low), GROUP, scatter_dimension=0, tiled=T...  53.6 us
    dot_general x6, matrix products, dot_rows(): lax.dot_general(first, second, (((1,), (1,)), ((), ())), preferred_elemen...  46.9 us
    reduce_scatter x1, waiting for transfers between devices, body(): lax.psum_scatter(dot_tokens(up_grad, norm_all).astype(low).reshape(owned,...  46 us
    all_gather x1, waiting for transfers between devices, body(): qkv_all = lax.all_gather(own_part(qkv_w), ALL, axis=0, tiled=True)  41.8 us
    reduce_scatter x1, waiting for transfers between devices, body(): lax.psum_scatter(rows_grad.astype(low), GROUP, scatter_dimension=0, tiled...  41.8 us
    reduce_scatter x1, waiting for transfers between devices, body(): lax.psum_scatter(dot_tokens(gate_grad, norm_all).astype(low).reshape(owne...  41.8 us
  transfers between devices with their start and end apart: 18, of which 16 were waited for; matrix products, arithmetic and copies ran while one was open for 11% of the time, Pallas kernels for 0%

profile of v1, /device:TPU:0, one launch (start us, length us, event | category | flops | bytes accessed | tf_op | source)
XLA Modules:
  0.0 1224.7 jit_solution(10965404914122239117)
XLA Ops:
  9.6 22.1 %all_gather.42 = bf16[2,1024]{1,0:T(2,128)(2,1)S(1)} all-gather(bf16[2,128]{1,0:T(2,128)(2,1)S(1)} %convert_element_type.155), channel_id=1, replica_groups=mesh['x'=2,'core'=2,'z'=4,'y'=2] {'z','y'}, dimensions={1}, use_global_device_ids=true | all-gather | bytes 4608 | tf_op jit(solution)/shard_map/all_gather | solution.py:103
  34.4 41.8 %all-gather.15.cloned.1.call-done = bf16[1024,2048]{1,0:T(8,128)(2,1)} async-done(((bf16[32,2048]{1,0:T(8,128)(2,1)}), bf16[1024,2048]{1,0:T(8,128)(2,1)}) %all-gather.15.cloned.1.call-update) | async-done | bytes 4194320 | tf_op jit(solution)/shard_map/all_gather | solution.py:102
  87.7 16.2 %all-gather.17.cloned.1.call-done = bf16[1024,1024]{1,0:T(8,128)(2,1)} async-done(((bf16[256,1024]{1,0:T(8,128)(2,1)}), bf16[1024,1024]{1,0:T(8,128)(2,1)}) %all-gather.17.cloned.1.call-update) | async-done | bytes 2097168 | tf_op jit(solution)/shard_map/all_gather | solution.py:131
  106.7 10.2 fusion.82
  128.3 35.5 %all-gather.19.cloned.1.call-done = bf16[1024,1024]{1,0:T(8,128)(2,1)} async-done(((bf16[32,1024]{1,0:T(8,128)(2,1)}), bf16[1024,1024]{1,0:T(8,128)(2,1)}) %all-gather.19.cloned.1.call-update) | async-done | bytes 2097168 | tf_op jit(solution)/shard_map/all_gather | solution.py:104
  173.8 40.0 %all-gather.4 = bf16[32,32,16]{1,2,0:T(8,128)(2,1)S(1)} all-gather(bf16[1,32,16]{1,2,0:T(8,128)(2,1)S(1)} %fusion.55), channel_id=1, replica_groups=mesh['x'=2,'core'=2,'z'=4,'y'=2] {'z','y','x','core'}, dimensions={0}, use_global_device_ids=true | all-gather | bytes 33792 | tf_op jit(solution)/shard_map/all_gather | solution.py:105
  214.0 15.9 %all-gather.2 = s32[1,2048,8]{1,2,0:T(8,128)S(1)} all-gather(s32[1,256,8]{1,2,0:T(8,128)S(1)} %copy-done.25), channel_id=4, replica_groups=mesh['x'=2,'core'=2,'z'=4,'y'=2] {'x','core','y'}, dimensions={1}, use_global_device_ids=true | all-gather | bytes 73728 | tf_op jit(solution)/shard_map/all_gather | solution.py:113
  233.6 17.8 %all-gather.25.cloned.1.call-done = bf16[4,1,256,1024]{3,2,1,0:T(8,128)(2,1)} async-done(((bf16[4,1,64,1024]{3,2,1,0:T(8,128)(2,1)}), bf16[4,1,256,1024]{3,2,1,0:T(8,128)(2,1)}) %all-gather.25.cloned.1.call-update) | async-done | bytes 2097168 | tf_op jit(solution)/shard_map/all_gather | solution.py:106
  251.4 10.6 fusion.84
  262.1 36.0 %all-gather.27.cloned.1.call-done = bf16[4,1,256,1024]{3,2,1,0:T(8,128)(2,1)} async-done(((bf16[4,1,64,1024]{3,2,1,0:T(8,128)(2,1)}), bf16[4,1,256,1024]{3,2,1,0:T(8,128)(2,1)}) %all-gather.27.cloned.1.call-update) | async-done | bytes 2097168 | tf_op jit(solution)/shard_map/all_gather | solution.py:107
  298.1 10.6 fusion.85
  308.8 36.2 %all-gather.23.cloned.1.call-done = bf16[4,256,1024]{2,1,0:T(8,128)(2,1)} async-done(((bf16[4,64,1024]{2,1,0:T(8,128)(2,1)}), bf16[4,256,1024]{2,1,0:T(8,128)(2,1)}) %all-gather.23.cloned.1.call-update) | async-done | bytes 2097168 | tf_op jit(solution)/shard_map/all_gather | solution.py:108
  345.0 37.4 %all-gather.29.cloned.1.call-done = bf16[1,2048,1024]{2,1,0:T(8,128)(2,1)} async-done(((bf16[1,256,1024]{2,1,0:T(8,128)(2,1)}), bf16[1,2048,1024]{2,1,0:T(8,128)(2,1)}) %all-gather.29.cloned.1.call-update) | async-done | bytes 4194320 | tf_op jit(solution)/shard_map/all_gather | solution.py:114
  382.4 17.0 %bitcast_reduce_fusion = (f32[2048,4]{0,1:T(4,128)S(1)}, f32[2048,1024]{0,1:T(8,128)}) fusion(f32[2048,1024]{0,1:T(8,128)} %fusion.85, f32[2048,1024]{0,1:T(8,128)} %fusion.84, bf16[1024,1024]{1,0:T(8,128)(2,1)} %bitcast.198, bf16[1,2048,1024]{2,1,0:T(8,128)(2,1)} %all-gather.29.cloned.1.call-done), kind=kOutput, calls=%fused_computation.13 | convolution fusion | flops 4309639168 | bytes 31490048 | tf_op jit(solution)/shard_map/dot_general | solution.py:157
  399.5 13.0 %multiply_convert_fusion = (bf16[2048,1024]{0,1:T(8,128)(2,1)}, bf16[2048,1024]{0,1:T(8,128)(2,1)}, bf16[2048,1024]{0,1:T(8,128)(2,1)}) fusion(f32[2048,1024]{0,1:T(8,128)S(1)} %bitcast.160, f32[2048,1024]{0,1:T(8,128)} %get-tuple-element.77, f32[2048,4]{0,1:T(4,128)S(1)} %get-tuple-element.43, f32[2048,1024]{0,1:T(8,128)} %fusion.85), kind=kLoop, calls=%fused_computation.15 | loop fusion | flops 37748736 | bytes 37781504 | tf_op jit(solution)/shard_map/convert_element_type | solution.py:183
  412.5 7.2 fusion.87
  427.9 9.4 convolution_convert_fusion.1
  437.4 41.8 %reduce-scatter.17.cloned.1.call-done = bf16[256,1024]{1,0:T(8,128)(2,1)} async-done(((bf16[2048,1024]{1,0:T(8,128)(2,1)}), bf16[256,1024]{1,0:T(8,128)(2,1)}) %reduce-scatter.17.cloned.1.call-update) | async-done | bytes 524304 | tf_op jit(solution)/shard_map/reduce_scatter | solution.py:193
  480.5 53.6 %reduce-scatter.15.cloned.1.call-done = bf16[256,1024]{1,0:T(8,128)(2,1)} async-done(((bf16[2048,1024]{1,0:T(8,128)(2,1)}), bf16[256,1024]{1,0:T(8,128)(2,1)}) %reduce-scatter.15.cloned.1.call-update) | async-done | bytes 524304 | tf_op jit(solution)/shard_map/reduce_scatter | solution.py:173
  543.4 7.0 bitcast_convert_fusion
  550.4 7.2 fusion.2
  567.0 9.8 fusion.17
  576.9 9.4 convolution_convert_fusion.3
  586.4 9.4 convolution_convert_fusion.2
  613.9 116.9 %reduce-scatter.31.cloned.1.call-done = bf16[32,16]{1,0:T(8,128)(2,1)} async-done(((bf16[1024,16]{1,0:T(8,128)(2,1)}), bf16[32,16]{1,0:T(8,128)(2,1)}) %reduce-scatter.31.cloned.1.call-update) | async-done | bytes 1040
  737.4 35.4 %reduce-scatter.29.cloned.1.call-done = bf16[4,64,1024]{2,1,0:T(8,128)(2,1)} async-done(((bf16[4,256,1024]{2,1,0:T(8,128)(2,1)}), bf16[4,64,1024]{2,1,0:T(8,128)(2,1)}) %reduce-scatter.29.cloned.1.call-update) | async-done | bytes 524304 | tf_op jit(solution)/shard_map/reduce_scatter | solution.py:176
  777.2 41.8 %reduce-scatter.25.cloned.1.call-done = bf16[4,64,1024]{2,1,0:T(8,128)(2,1)} async-done(((bf16[4,256,1024]{2,1,0:T(8,128)(2,1)}), bf16[4,64,1024]{2,1,0:T(8,128)(2,1)}) %reduce-scatter.25.cloned.1.call-update) | async-done | bytes 524304 | tf_op jit(solution)/shard_map/reduce_scatter | solution.py:196
  818.9 46.0 %reduce-scatter.27.cloned.1.call-done = bf16[4,64,1024]{2,1,0:T(8,128)(2,1)} async-done(((bf16[4,256,1024]{2,1,0:T(8,128)(2,1)}), bf16[4,64,1024]{2,1,0:T(8,128)(2,1)}) %reduce-scatter.27.cloned.1.call-update) | async-done | bytes 524304 | tf_op jit(solution)/shard_map/reduce_scatter | solution.py:202
  871.5 131.7 %reduce-scatter.23.cloned.1.call-done = bf16[32,1024]{1,0:T(8,128)(2,1)} async-done(((bf16[1024,1024]{1,0:T(8,128)(2,1)}), bf16[32,1024]{1,0:T(8,128)(2,1)}) %reduce-scatter.23.cloned.1.call-update) | async-done | bytes 65552 | tf_op jit(solution)/shard_map/reduce_scatter | solution.py:245
  1014.3 50.5 %reduce-scatter.33.cloned.1.call-done = f32[128,2]{1,0:T(8,128)} async-done(((f32[1024,2]{1,0:T(8,128)}), f32[128,2]{1,0:T(8,128)}) %reduce-scatter.33.cloned.1.call-update) | async-done | bytes 1040
  1071.9 135.0 %reduce-scatter.21.cloned.1.call-done = bf16[32,2048]{1,0:T(8,128)(2,1)} async-done(((bf16[1024,2048]{1,0:T(8,128)(2,1)}), bf16[32,2048]{1,0:T(8,128)(2,1)}) %reduce-scatter.21.cloned.1.call-update) | async-done | bytes 131088 | tf_op jit(solution)/shard_map/reduce_scatter | solution.py:245
  1206.9 6.7 all_gather.53
  (195 shorter events, 130.1 us)
Async XLA Ops:
  7.2 69.0 %all-gather.15.cloned.1.call-start = ((), (), s32[]{:S(2)}) async-start(), calls=%async_computation.10 | async-start | bytes 4325376 | tf_op jit(solution)/shard_map/all_gather | solution.py:102
  8.9 95.1 %all-gather.17.cloned.1.call-start = ((), (), s32[]{:S(2)}) async-start(), calls=%async_computation.11 | async-start | bytes 2621440 | tf_op jit(solution)/shard_map/all_gather | solution.py:131
  33.6 47.7 %copy-start.29 = (f32[256]{0:T(256)}, f32[256]{0:T(256)S(1)}, u32[]{:S(2)}) copy-start(f32[256]{0:T(256)S(1)} %get-tuple-element.69) | copy-start | bytes 3076
  33.6 47.7 %copy-start.23 = (f32[1,1024]{1,0:T(1,128)}, f32[1,1024]{1,0:T(1,128)S(1)}, u32[]{:S(2)}) copy-start(f32[1,1024]{1,0:T(1,128)S(1)} %get-tuple-element.64) | copy-start | bytes 12292
  34.4 52.4 %copy-start.18 = (f32[256,32]{0,1:T(8,128)}, f32[256,32]{0,1:T(8,128)S(1)}, u32[]{:S(2)}) copy-start(f32[256,32]{0,1:T(8,128)S(1)} %get-tuple-element.67) | copy-start | bytes 98308
  82.7 81.1 %all-gather.19.cloned.1.call-start = ((), (), s32[]{:S(2)}) async-start(), calls=%async_computation.12 | async-start | bytes 2162688 | tf_op jit(solution)/shard_map/all_gather | solution.py:104
  84.3 145.8 %all-gather.21.cloned.1.call-start = ((), (), s32[]{:S(2)}) async-start(), calls=%async_computation.13 | async-start | bytes 4718592 | tf_op jit(solution)/shard_map/all_gather | solution.py:147
  167.2 84.2 %all-gather.25.cloned.1.call-start = ((), (), s32[]{:S(2)}) async-start(), calls=%async_computation.23 | async-start | bytes 2621440 | tf_op jit(solution)/shard_map/all_gather | solution.py:106
  170.2 128.0 %all-gather.27.cloned.1.call-start = ((), (), s32[]{:S(2)}) async-start(), calls=%async_computation.24 | async-start | bytes 2621440 | tf_op jit(solution)/shard_map/all_gather | solution.py:107
  170.7 174.2 %all-gather.23.cloned.1.call-start = ((), (), s32[]{:S(2)}) async-start(), calls=%async_computation.14 | async-start | bytes 2621440 | tf_op jit(solution)/shard_map/all_gather | solution.py:108
  172.9 209.5 %all-gather.29.cloned.1.call-start = ((), (), s32[]{:S(2)}) async-start(), calls=%async_computation.25 | async-start | bytes 4718592 | tf_op jit(solution)/shard_map/all_gather | solution.py:114
  173.7 305.5 %reduce-scatter.17.cloned.1.call-start = ((), (), s32[]{:S(2)}) async-start(), calls=%async_computation.16 | async-start | bytes 4718592 | tf_op jit(solution)/shard_map/reduce_scatter | solution.py:193
  427.7 106.4 %reduce-scatter.15.cloned.1.call-start = ((), (), s32[]{:S(2)}) async-start(), calls=%async_computation.15 | async-start | bytes 4718592 | tf_op jit(solution)/shard_map/reduce_scatter | solution.py:173
  437.3 96.8 %copy-start.14 = (bf16[1,256,1024]{2,1,0:T(8,128)(2,1)S(1)}, bf16[1,256,1024]{2,1,0:T(8,128)(2,1)}, u32[]{:S(2)}) copy-start(bf16[1,256,1024]{2,1,0:T(8,128)(2,1)} %param.22) | copy-start | bytes 1572868
  437.3 166.2 %reduce-scatter.19.cloned.1.call-start = ((), (), s32[]{:S(2)}) async-start(), calls=%async_computation.17 | async-start | bytes 2621440 | tf_op jit(solution)/shard_map/reduce_scatter | solution.py:231
  563.0 167.8 %reduce-scatter.31.cloned.1.call-start = ((), (), s32[]{:S(2)}) async-start(), calls=%async_computation.26 | async-start | bytes 270336
  566.8 206.1 %reduce-scatter.29.cloned.1.call-start = ((), (), s32[]{:S(2)}) async-start(), calls=%async_computation.22 | async-start | bytes 2621440 | tf_op jit(solution)/shard_map/reduce_scatter | solution.py:176
  576.9 242.1 %reduce-scatter.25.cloned.1.call-start = ((), (), s32[]{:S(2)}) async-start(), calls=%async_computation.20 | async-start | bytes 2621440 | tf_op jit(solution)/shard_map/reduce_scatter | solution.py:196
  586.3 278.6 %reduce-scatter.27.cloned.1.call-start = ((), (), s32[]{:S(2)}) async-start(), calls=%async_computation.21 | async-start | bytes 2621440 | tf_op jit(solution)/shard_map/reduce_scatter | solution.py:202
  595.8 407.4 %reduce-scatter.23.cloned.1.call-start = ((), (), s32[]{:S(2)}) async-start(), calls=%async_computation.19 | async-start | bytes 2162688 | tf_op jit(solution)/shard_map/reduce_scatter | solution.py:245
  598.0 466.7 %reduce-scatter.33.cloned.1.call-start = ((), (), s32[]{:S(2)}) async-start(), calls=%async_computation.27 | async-start | bytes 589824
  610.3 126.5 %copy-start.22 = (f32[128,16]{0,1:T(8,128)S(1)}, f32[128,16]{0,1:T(8,128)}, u32[]{:S(2)}) copy-start(f32[128,16]{0,1:T(8,128)} %param.30) | copy-start | bytes 24580
  610.4 126.4 %copy-start.26 = (f32[128,16]{0,1:T(8,128)S(1)}, f32[128,16]{0,1:T(8,128)}, u32[]{:S(2)}) copy-start(f32[128,16]{0,1:T(8,128)} %param.32) | copy-start | bytes 24580
  610.4 126.4 %copy-start.27 = (f32[128,16]{0,1:T(8,128)S(1)}, f32[128,16]{0,1:T(8,128)}, u32[]{:S(2)}) copy-start(f32[128,16]{0,1:T(8,128)} %param.31) | copy-start | bytes 24580
  610.4 596.6 %reduce-scatter.21.cloned.1.call-start = ((), (), s32[]{:S(2)}) async-start(), calls=%async_computation.18 | async-start | bytes 4325376 | tf_op jit(solution)/shard_map/reduce_scatter | solution.py:245
  613.9 251.0 %copy-start.5 = (f32[4,2,64,1024]{3,2,1,0:T(8,128)S(1)}, f32[4,2,64,1024]{3,2,1,0:T(8,128)}, u32[]{:S(2)}) copy-start(f32[4,2,64,1024]{3,2,1,0:T(8,128)} %param.36) | copy-start | bytes 6291460
  864.9 147.1 %copy-start.28 = (f32[256]{0:T(256)S(1)}, f32[256]{0:T(256)}, u32[]{:S(2)}) copy-start(f32[256]{0:T(256)} %get-tuple-element.68) | copy-start | bytes 3076
  871.5 140.5 %copy-start.17 = (f32[256,1024]{1,0:T(8,128)S(1)}, f32[256,1024]{1,0:T(8,128)}, u32[]{:S(2)}) copy-start(f32[256,1024]{1,0:T(8,128)} %get-tuple-element.82) | copy-start | bytes 3145732
  871.5 199.9 %copy-start.31 = (f32[2,128]{1,0:T(2,128)S(1)}, f32[2,128]{1,0:T(2,128)}, u32[]{:S(2)}) copy-start(f32[2,128]{1,0:T(2,128)} %param.33) | copy-start | bytes 3076
  871.5 199.9 %copy-start.32 = (f32[2,128]{1,0:T(2,128)S(1)}, f32[2,128]{1,0:T(2,128)}, u32[]{:S(2)}) copy-start(f32[2,128]{1,0:T(2,128)} %param.35) | copy-start | bytes 3076
  871.5 199.9 %copy-start.33 = (f32[2,128]{1,0:T(2,128)S(1)}, f32[2,128]{1,0:T(2,128)}, u32[]{:S(2)}) copy-start(f32[2,128]{1,0:T(2,128)} %param.34) | copy-start | bytes 3076
  871.5 342.2 %copy-start.16 = (f32[128,2048]{1,0:T(8,128)S(1)}, f32[128,2048]{1,0:T(8,128)}, u32[]{:S(2)}) copy-start(f32[128,2048]{1,0:T(8,128)} %param.24) | copy-start | bytes 3145732
  (23 other events, 243.8 us)
Sparse Core Ops, SparseCore 0:
  11.5 64.7 all-gather.14
  82.8 21.1 all-gather.16
  107.4 56.3 all-gather.18
  167.3 36.1 all-gather.20
  205.5 45.9 all-gather.24
  253.4 44.6 all-gather.26
  300.3 44.6 all-gather.22
  346.8 35.4 all-gather.28
  427.8 51.3 reduce-scatter.16
  482.7 51.3 reduce-scatter.14
  563.1 31.3 reduce-scatter.18
  597.3 133.4 reduce-scatter.30
  733.1 39.7 reduce-scatter.28
  775.7 43.1 reduce-scatter.24
  821.6 43.1 reduce-scatter.26
  867.1 136.0 reduce-scatter.22
  1006.9 57.8 reduce-scatter.32
  1067.0 139.8 reduce-scatter.20

commit v2 on v1

v2 whole, which is shorter than its diff:
```python
import functools
import math

import jax
import jax.numpy as jnp
from jax import lax
from jax.experimental import pallas as pl
from jax.experimental.pallas import tpu as pltpu
from jax.sharding import PartitionSpec as P

D = 1024
HQ = 16
KVH = 8
HD = 64
FF = 512
STEP = 10

EXPERT = ("x", "core")
SHARD = ("z", "y")
EXTRA = 16
TILE = 256

beta_one = 0.9
beta_two = 0.95
adam_eps = 1e-08
weight_decay = 0.1
norm_eps = 1e-05
rope_base = 10000.0
masked_score = -1e30
low = jnp.bfloat16
high = jnp.float32

SMALL = pl.BlockSpec(memory_space=pltpu.SMEM)
WHOLE = pl.BlockSpec(memory_space=pltpu.VMEM)
PARAMS = pltpu.CompilerParams(vmem_limit_bytes=56 * 1024 * 1024)


def rms_scale(values):
    return lax.rsqrt(jnp.mean(values * values, axis=-1, keepdims=True) + norm_eps)


def norm_back(values, scale, gain, grad):
    weighted = gain * grad
    inner = jnp.mean(values * weighted, axis=-1, keepdims=True)
    return scale * weighted - values * (scale * scale * scale) * inner


def dot_plain(first, second):
    return jnp.dot(first, second, preferred_element_type=high)


def dot_rows(first, second):
    return lax.dot_general(first, second, (((1,), (1,)), ((), ())), preferred_element_type=high)


def dot_tokens(first, second):
    return lax.dot_general(first, second, (((0,), (0,)), ((), ())), preferred_element_type=high)


def adam_step(weight, first, second, grad, rate, decay):
    new_first = beta_one * first + (1.0 - beta_one) * grad
    new_second = beta_two * second + (1.0 - beta_two) * grad * grad
    fix_one = 1.0 - beta_one**STEP
    fix_two = 1.0 - beta_two**STEP
    update = new_first / fix_one / (jnp.sqrt(new_second / fix_two) + adam_eps)
    return (new_first, new_second, weight - rate * (update + decay * weight))


def rotary_tables(length):
    half = HD // 2
    freqs = rope_base ** (-jnp.arange(half, dtype=high) / half)
    angles = jnp.arange(length, dtype=high)[:, None] * freqs[None, :]
    cosine = jnp.cos(angles)
    sine = jnp.sin(angles)
    return (
        jnp.concatenate([cosine] * 4, axis=1),
        jnp.concatenate([-sine, sine, -sine, sine], axis=1),
    )


def rotary(values, cosine, sine, turned):
    blocks = []
    for start in range(0, values.shape[1], 128):
        block = values[:, start : start + 128]
        count = min(128, turned - start)
        if count > 0:
            lane = lax.broadcasted_iota(jnp.int32, block.shape, 1)
            partner = jnp.where(
                lane % HD < HD // 2,
                pltpu.roll(block, 128 - HD // 2, axis=1),
                pltpu.roll(block, HD // 2, axis=1),
            )
            moved = block * cosine + partner * sine
            block = moved if count == 128 else jnp.where(lane < count, moved, block)
        blocks.append(block)
    return jnp.concatenate(blocks, axis=1)


def causal_tail(scores, filler):
    tile, keys = scores.shape
    row = lax.broadcasted_iota(jnp.int32, scores.shape, 0)
    column = lax.broadcasted_iota(jnp.int32, scores.shape, 1)
    return jnp.where(column <= row + (keys - tile), scores, filler)


def attend_kernel(
    heads,
    keys,
    slots,
    shards,
    x_ref,
    w_ref,
    cos_ref,
    sin_ref,
    norm_ref,
    weight_ref,
    extra_ref,
    query_ref,
    key_ref,
    value_ref,
    out_ref,
    total_ref,
    head_out,
):
    count, rows, width = x_ref.shape
    length = count * rows
    part = w_ref.shape[1] - EXTRA
    for shard in range(w_ref.shape[0]):
        place = slice(shard * part, (shard + 1) * part)
        slot = shards[shard]
        weight_ref[place, :] = w_ref[slot, :part, :]
        extra_ref[:EXTRA, place] = w_ref[slot, part:, :part]
        extra_ref[EXTRA:, place] = w_ref[slot, part:, part : 2 * part]
    gain = extra_ref[EXTRA : EXTRA + 1, :].astype(high)
    for block in range(count):
        place = slice(block * rows, (block + 1) * rows)
        values = x_ref[slots[block]].astype(high)
        normed = (values * rms_scale(values) * gain).astype(low)
        norm_ref[place, :] = normed
        proj = rotary(
            dot_plain(normed, weight_ref[...]),
            cos_ref[place, :],
            sin_ref[place, :],
            (heads + keys) * HD,
        )
        for head in range(heads):
            query_ref[head, place, :] = (proj[:, head * HD : (head + 1) * HD] * 0.125).astype(low)
        for head in range(keys):
            start = (heads + head) * HD
            key_ref[head, place, :] = proj[:, start : start + HD].astype(low)
            start = (heads + keys + head) * HD
            value_ref[head, place, :] = proj[:, start : start + HD].astype(low)

    def one_head(head, carry):
        group = lax.div(head, heads // keys)
        for tile in range(length // TILE):
            place = slice(tile * TILE, (tile + 1) * TILE)
            seen = (tile + 1) * TILE
            scores = dot_rows(query_ref[head, place, :], key_ref[group, :seen, :])
            scores = causal_tail(scores, masked_score)
            peak = jnp.max(scores, axis=-1, keepdims=True)
            weights = jnp.exp(scores - peak)
            total = jnp.sum(weights, axis=-1, keepdims=True)
            total_ref[head, place, :] = peak + jnp.log(total)
            summed = dot_plain(weights.astype(low), value_ref[group, :seen, :])
            head_out[head, place, :] = summed / total
        return carry

    lax.fori_loop(0, heads, one_head, 0)
    for head in range(heads):
        out_ref[:, head * HD : (head + 1) * HD] = head_out[head].astype(low)


def attend(slots, shards, x_all, w_all, cosine, sine, heads, keys):
    count, rows, width = x_all.shape
    length = count * rows
    columns = w_all.shape[2]
    return pl.pallas_call(
        functools.partial(attend_kernel, heads, keys),
        out_shape=(
            jax.ShapeDtypeStruct((length, width), low),
            jax.ShapeDtypeStruct((width, columns), low),
            jax.ShapeDtypeStruct((2 * EXTRA, width), low),
            jax.ShapeDtypeStruct((heads, length, HD), low),
            jax.ShapeDtypeStruct((keys, length, HD), low),
            jax.ShapeDtypeStruct((keys, length, HD), low),
            jax.ShapeDtypeStruct((length, heads * HD), low),
            jax.ShapeDtypeStruct((heads, length, 1), high),
        ),
        in_specs=[SMALL, SMALL, WHOLE, WHOLE, WHOLE, WHOLE],
        out_specs=[WHOLE] * 8,
        scratch_shapes=[pltpu.VMEM((heads, length, HD), high)],
        compiler_params=PARAMS,
        cost_estimate=pl.CostEstimate(
            flops=2 * length * width * columns + 3 * length * length * heads * HD,
            bytes_accessed=12 << 20,
            transcendentals=length * length * heads // 2,
        ),
        name="attend",
    )(slots, shards, x_all, w_all, cosine, sine)


def project_kernel(slots, sides, o_ref, w_ref, out_ref, weight):
    part = w_ref.shape[1]
    for side in range(w_ref.shape[0]):
        weight[side * part : (side + 1) * part, :] = w_ref[sides[side]]
    count, rows, _ = out_ref.shape
    for block in range(count):
        out_ref[slots[block]] = dot_plain(
            o_ref[block * rows : (block + 1) * rows, :], weight[...]
        ).astype(low)


def project(slots, sides, attended, w_all, count):
    length, inner = attended.shape
    width = w_all.shape[2]
    return pl.pallas_call(
        project_kernel,
        out_shape=jax.ShapeDtypeStruct((count, length // count, width), low),
        in_specs=[SMALL, SMALL, WHOLE, WHOLE],
        out_specs=WHOLE,
        scratch_shapes=[pltpu.VMEM((inner, width), low)],
        compiler_params=PARAMS,
        cost_estimate=pl.CostEstimate(
            flops=2 * length * inner * width, bytes_accessed=3 << 20, transcendentals=0
        ),
        name="project",
    )(slots, sides, attended, w_all)


def experts_kernel(
    first,
    h_ref,
    pack_ref,
    router_ref,
    gate_ref,
    up_ref,
    down_ref,
    act_ref,
    gate_grad_ref,
    up_grad_ref,
    logit_ref,
    down_grad_ref,
    router_grad_ref,
    down_sum,
    router_sum,
):
    step = pl.program_id(0)
    owned, hidden, width = gate_ref.shape
    experts = router_ref.shape[0]

    @pl.when(step == 0)
    def _():
        down_sum[...] = jnp.zeros_like(down_sum)
        router_sum[...] = jnp.zeros_like(router_sum)

    rows = h_ref[...]
    grads = pack_ref[:, :width]
    chosen = pack_ref[:, width : width + experts].astype(high) > 0.5
    logits = jnp.where(chosen, dot_rows(rows, router_ref[...]), masked_score)
    powers = jnp.exp(logits - jnp.max(logits, axis=-1, keepdims=True))
    powers = jnp.where(chosen, powers, 0.0)
    gates = powers / jnp.sum(powers, axis=-1, keepdims=True)
    lane = lax.broadcasted_iota(jnp.int32, gates.shape, 1)

    def one_expert(expert, gate_grads):
        mine = lane == first[0] + expert
        gate = jnp.sum(jnp.where(mine, gates, 0.0), axis=1, keepdims=True)
        place = pl.ds(pl.multiple_of(expert * hidden, 128), hidden)
        gate_part = dot_rows(rows, gate_ref[expert])
        up_part = dot_rows(rows, up_ref[expert])
        plain = dot_rows(grads, down_ref[expert])
        sigmoid = 1.0 / (1.0 + jnp.exp(-gate_part))
        swish = gate_part * sigmoid
        active = swish * up_part
        found = jnp.sum(plain * active, axis=1, keepdims=True) * gate
        weighted = (active * gate).astype(low)
        plain = plain * gate
        act_ref[:, place] = weighted
        gate_grad_ref[:, place] = (
            plain * up_part * (sigmoid + swish * (1.0 - sigmoid))
        ).astype(low)
        up_grad_ref[:, place] = (plain * swish).astype(low)
        down_sum[expert] += dot_tokens(weighted, grads)
        return gate_grads + jnp.where(mine, found, 0.0)

    gate_grads = lax.fori_loop(0, owned, one_expert, jnp.zeros_like(gates))
    logit_grads = gate_grads - gates * jnp.sum(gate_grads, axis=1, keepdims=True)
    logit_grads = logit_grads.astype(low)
    logit_ref[...] = logit_grads
    router_sum[...] += dot_tokens(logit_grads, rows)

    @pl.when(step == pl.num_programs(0) - 1)
    def _():
        down_grad_ref[...] = down_sum[...].astype(low)
        router_grad_ref[...] = router_sum[...]


def run_experts(first, h_all, pack_all, router, gate_w, up_w, down_w):
    count, width = h_all.shape
    owned, hidden, _ = gate_w.shape
    experts = router.shape[0]
    tile = 512
    inner = owned * hidden

    def by_tile(columns):
        return pl.BlockSpec((tile, columns), lambda i: (i, 0))

    def fixed(*shape):
        return pl.BlockSpec(shape, lambda i: (0,) * len(shape))

    return pl.pallas_call(
        experts_kernel,
        grid=(count // tile,),
        out_shape=(
            jax.ShapeDtypeStruct((count, inner), low),
            jax.ShapeDtypeStruct((count, inner), low),
            jax.ShapeDtypeStruct((count, inner), low),
            jax.ShapeDtypeStruct((count, experts), low),
            jax.ShapeDtypeStruct((owned, hidden, width), low),
            jax.ShapeDtypeStruct((experts, width), high),
        ),
        in_specs=[
            SMALL,
            by_tile(width),
            by_tile(pack_all.shape[1]),
            fixed(experts, width),
            fixed(owned, hidden, width),
            fixed(owned, hidden, width),
            fixed(owned, hidden, width),
        ],
        out_specs=(
            by_tile(inner),
            by_tile(inner),
            by_tile(inner),
            by_tile(experts),
            fixed(owned, hidden, width),
            fixed(experts, width),
        ),
        scratch_shapes=[
            pltpu.VMEM((owned, hidden, width), high),
            pltpu.VMEM((experts, width), high),
        ],
        compiler_params=PARAMS,
        cost_estimate=pl.CostEstimate(
            flops=8 * count * inner * width, bytes_accessed=30 << 20, transcendentals=count * inner
        ),
        name="experts",
    )(first, h_all, pack_all, router, gate_w, up_w, down_w)


def back_rows_kernel(gate_grad_ref, up_grad_ref, logit_ref, gate_ref, up_ref, router_ref, out_ref):
    out_ref[...] = (
        dot_plain(gate_grad_ref[...], gate_ref[...])
        + dot_plain(up_grad_ref[...], up_ref[...])
        + dot_plain(logit_ref[...], router_ref[...])
    ).astype(low)


def back_rows(gate_grad, up_grad, logit_grad, gate_w, up_w, router):
    count, inner = gate_grad.shape
    width = gate_w.shape[1]
    experts = router.shape[0]
    tile = 512
    return pl.pallas_call(
        back_rows_kernel,
        grid=(count // tile,),
        out_shape=jax.ShapeDtypeStruct((count, width), low),
        in_specs=[
            pl.BlockSpec((tile, inner), lambda i: (i, 0)),
            pl.BlockSpec((tile, inner), lambda i: (i, 0)),
            pl.BlockSpec((tile, experts), lambda i: (i, 0)),
            pl.BlockSpec((inner, width), lambda i: (0, 0)),
            pl.BlockSpec((inner, width), lambda i: (0, 0)),
            pl.BlockSpec((experts, width), lambda i: (0, 0)),
        ],
        out_specs=pl.BlockSpec((tile, width), lambda i: (i, 0)),
        compiler_params=PARAMS,
        cost_estimate=pl.CostEstimate(
            flops=4 * count * inner * width, bytes_accessed=16 << 20, transcendentals=0
        ),
        name="back_rows",
    )(gate_grad, up_grad, logit_grad, gate_w, up_w, router)


def weight_grads_kernel(gate_grad_ref, up_grad_ref, h_ref, gate_ref, up_ref):
    gate_ref[...] = dot_tokens(gate_grad_ref[...], h_ref[...]).astype(low)
    up_ref[...] = dot_tokens(up_grad_ref[...], h_ref[...]).astype(low)


def weight_grads(gate_grad, up_grad, h_all):
    count, inner = gate_grad.shape
    width = h_all.shape[1]
    block = 256
    return pl.pallas_call(
        weight_grads_kernel,
        grid=(inner // block,),
        out_shape=(jax.ShapeDtypeStruct((inner, width), low),) * 2,
        in_specs=[
            pl.BlockSpec((count, block), lambda i: (0, i)),
            pl.BlockSpec((count, block), lambda i: (0, i)),
            pl.BlockSpec((count, width), lambda i: (0, 0)),
        ],
        out_specs=(pl.BlockSpec((block, width), lambda i: (i, 0)),) * 2,
        compiler_params=PARAMS,
        cost_estimate=pl.CostEstimate(
            flops=4 * count * inner * width, bytes_accessed=16 << 20, transcendentals=0
        ),
        name="weight_grads",
    )(gate_grad, up_grad, h_all)


def results_kernel(act_ref, down_ref, out_ref):
    out_ref[...] = dot_plain(act_ref[...], down_ref[...]).astype(low)


def expert_results(act, down_w):
    count, inner = act.shape
    width = down_w.shape[1]
    tile = 512
    return pl.pallas_call(
        results_kernel,
        grid=(count // tile,),
        out_shape=jax.ShapeDtypeStruct((count, width), low),
        in_specs=[
            pl.BlockSpec((tile, inner), lambda i: (i, 0)),
            pl.BlockSpec((inner, width), lambda i: (0, 0)),
        ],
        out_specs=pl.BlockSpec((tile, width), lambda i: (i, 0)),
        compiler_params=PARAMS,
        cost_estimate=pl.CostEstimate(
            flops=2 * count * inner * width, bytes_accessed=10 << 20, transcendentals=0
        ),
        name="expert_results",
    )(act, down_w)


def attend_back_kernel(
    heads,
    keys,
    slots,
    shards,
    sides,
    grad_ref,
    x_ref,
    w_ref,
    weight_ref,
    norm_ref,
    query_ref,
    key_ref,
    value_ref,
    o_ref,
    total_ref,
    cos_ref,
    sin_ref,
    router_ref,
    gain_ref,
    qkv_ref,
    out_grad_ref,
    row_ref,
    out_w,
    out_sum,
    head_grad,
    head_o,
    query_sum,
    key_sum,
    value_sum,
    proj,
    proj_low,
    gains,
):
    count, rows, width = x_ref.shape
    length = count * rows
    part = w_ref.shape[1]
    for side in range(w_ref.shape[0]):
        out_w[side * part : (side + 1) * part, :] = w_ref[sides[side]]
    for block in range(count):
        place = slice(block * rows, (block + 1) * rows)
        grad = grad_ref[slots[block]]
        spread = dot_rows(grad, out_w[...]).astype(low)
        attended = o_ref[place, :]
        for head in range(heads):
            head_grad[head, place, :] = spread[:, head * HD : (head + 1) * HD]
            head_o[head, place, :] = attended[:, head * HD : (head + 1) * HD]
        piece = dot_tokens(attended, grad)
        out_sum[...] = piece if block == 0 else out_sum[...] + piece
    for side in range(w_ref.shape[0]):
        out_grad_ref[sides[side]] = out_sum[side * part : (side + 1) * part, :].astype(low)
    key_sum[...] = jnp.zeros_like(key_sum)
    value_sum[...] = jnp.zeros_like(value_sum)

    def one_head(head, carry):
        group = lax.div(head, heads // keys)
        for tile in range(length // TILE):
            place = slice(tile * TILE, (tile + 1) * TILE)
            seen = (tile + 1) * TILE
            query = query_ref[head, place, :]
            key = key_ref[group, :seen, :]
            grad = head_grad[head, place, :]
            scores = dot_rows(query, key) - total_ref[head, place, :]
            probs = jnp.exp(causal_tail(scores, masked_score))
            offset = jnp.sum(
                grad.astype(high) * head_o[head, place, :].astype(high), axis=-1, keepdims=True
            )
            inner = dot_rows(grad, value_ref[group, :seen, :])
            score_grad = (probs * (inner - offset)).astype(low)
            query_sum[head, place, :] = dot_plain(score_grad, key) * 0.125
            key_sum[group, :seen, :] += dot_tokens(score_grad, query)
            value_sum[group, :seen, :] += dot_tokens(probs.astype(low), grad)
        return carry

    lax.fori_loop(0, heads, one_head, 0)
    for head in range(heads):
        proj[:, head * HD : (head + 1) * HD] = query_sum[head]
    for head in range(keys):
        start = (heads + head) * HD
        proj[:, start : start + HD] = key_sum[head]
        start = (heads + keys + head) * HD
        proj[:, start : start + HD] = value_sum[head]
    gains[...] = jnp.zeros_like(gains)
    gains[1:2, :] = gain_ref[...]
    for block in range(count):
        place = slice(block * rows, (block + 1) * rows)
        turned = rotary(
            proj[place, :], cos_ref[place, :], -sin_ref[place, :], (heads + keys) * HD
        ).astype(low)
        proj_low[place, :] = turned
        back = dot_rows(turned, weight_ref[...])
        row_ref[slots[block]] = back.astype(low)
        values = x_ref[slots[block]].astype(high)
        gains[0:1, :] += jnp.sum(back * (values * rms_scale(values)), axis=0, keepdims=True)
    shard_count = qkv_ref.shape[0]
    for start in range(0, width, TILE):
        piece = dot_tokens(norm_ref[:, start : start + TILE], proj_low[...]).astype(low)
        for shard in range(start // part, (start + TILE) // part):
            offset = shard * part - start
            qkv_ref[shards[shard], :part, :] = piece[offset : offset + part, :]
    for shard in range(shard_count):
        place = slice(shard * part, (shard + 1) * part)
        slot = shards[shard]
        qkv_ref[slot, part:, :] = jnp.zeros((EXTRA, qkv_ref.shape[2]), low)
        qkv_ref[slot, part:, :part] = router_ref[:, place].astype(low)
        qkv_ref[slot, part:, part : 2 * part] = gains[:, place].astype(low)


def attend_back(
    slots,
    shards,
    sides,
    grad_all,
    x_all,
    w_all,
    weight,
    normed,
    query,
    key,
    value,
    attended,
    totals,
    cosine,
    sine,
    router_grad,
    gain_grad,
):
    count, rows, width = x_all.shape
    length = count * rows
    heads = query.shape[0]
    keys = key.shape[0]
    columns = weight.shape[1]
    part = w_all.shape[1]
    return pl.pallas_call(
        functools.partial(attend_back_kernel, heads, keys),
        out_shape=(
            jax.ShapeDtypeStruct((width // part, part + EXTRA, columns), low),
            jax.ShapeDtypeStruct(w_all.shape, low),
            jax.ShapeDtypeStruct(x_all.shape, low),
        ),
        in_specs=[SMALL] * 3 + [WHOLE] * 14,
        out_specs=[WHOLE] * 3,
        scratch_shapes=[
            pltpu.VMEM((heads * HD, width), low),
            pltpu.VMEM((heads * HD, width), high),
            pltpu.VMEM((heads, length, HD), low),
            pltpu.VMEM((heads, length, HD), low),
            pltpu.VMEM((heads, length, HD), high),
            pltpu.VMEM((keys, length, HD), high),
            pltpu.VMEM((keys, length, HD), high),
            pltpu.VMEM((length, columns), high),
            pltpu.VMEM((length, columns), low),
            pltpu.VMEM((EXTRA, width), high),
        ],
        compiler_params=PARAMS,
        cost_estimate=pl.CostEstimate(
            flops=4 * length * width * (columns + heads * HD) + 6 * length * length * heads * HD,
            bytes_accessed=20 << 20,
            transcendentals=length * length * heads // 2,
        ),
        name="attend_back",
    )(
        slots,
        shards,
        sides,
        grad_all,
        x_all,
        w_all,
        weight,
        normed,
        query,
        key,
        value,
        attended,
        totals,
        cosine,
        sine,
        router_grad,
        gain_grad,
    )


def qkv_step_kernel(rate, slots, g_ref, w_ref, m_ref, v_ref, m_out, v_out, w_out, extra_ref):
    count, whole, columns = g_ref.shape
    part = whole - EXTRA
    query = HQ * HD // count
    other = KVH * HD // count
    spans = (
        (0, query, 0),
        (query, other, HQ * HD),
        (query + other, other, HQ * HD + KVH * HD),
    )
    total = jnp.zeros((EXTRA, columns), high)
    for block in range(count):
        slot = slots[block]
        total = total + g_ref[slot, part:, :].astype(high)
        for start, size, base in spans:
            place = slice(base + block * size, base + (block + 1) * size)
            first, second, weight = adam_step(
                w_ref[:, place],
                m_ref[:, place],
                v_ref[:, place],
                g_ref[slot, :part, start : start + size].astype(high),
                rate,
                weight_decay,
            )
            m_out[:, place] = first
            v_out[:, place] = second
            w_out[:, place] = weight
    extra_ref[...] = total


def qkv_step(rate, slots, grads, weight, first, second):
    like = jax.ShapeDtypeStruct(weight.shape, high)
    return pl.pallas_call(
        functools.partial(qkv_step_kernel, rate),
        out_shape=(like, like, like, jax.ShapeDtypeStruct((EXTRA, grads.shape[2]), high)),
        in_specs=[SMALL] + [WHOLE] * 4,
        out_specs=[WHOLE] * 4,
        compiler_params=PARAMS,
        cost_estimate=pl.CostEstimate(
            flops=16 * weight.size, bytes_accessed=24 * weight.size, transcendentals=weight.size
        ),
        name="qkv_step",
    )(slots, grads, weight, first, second)


def shifted(value, axis, step):
    size = lax.axis_size(axis)
    return lax.ppermute(value, axis, [(j, (j + step) % size) for j in range(size)])


def collect(value, axis):
    size = lax.axis_size(axis)
    return jnp.stack([value] + [shifted(value, axis, step) for step in range(1, size)])


def give_back(pieces, axis):
    size = lax.axis_size(axis)
    total = pieces[0].astype(high)
    for step in range(1, size):
        total = total + shifted(pieces[step], axis, -step).astype(high)
    return total.astype(low)


def collect_group(value):
    half = value.shape[0] // 2
    width = value.shape[1]
    upper = collect(collect(value[:half], "x"), "y").reshape(-1, width)
    lower = collect(collect(value[half:], "y"), "x").reshape(-1, width)
    return collect(jnp.concatenate([upper, lower], axis=0), "core").reshape(-1, width)


def give_back_group(rows):
    total, width = rows.shape
    spread = lax.axis_size("x")
    sides = lax.axis_size("y")
    chip = give_back(rows.reshape(2, total // 2, width), "core")
    upper = chip[: total // 4].reshape(sides, spread, -1, width)
    lower = chip[total // 4 :].reshape(spread, sides, -1, width)
    upper = give_back(give_back(upper, "y"), "x")
    lower = give_back(give_back(lower, "x"), "y")
    return jnp.concatenate([upper, lower], axis=0)


def collect_expert(value):
    pieces = collect(collect(value, "x"), "core")
    return pieces.reshape((-1,) + value.shape)


def give_back_expert(pieces):
    pieces = pieces.reshape((2, pieces.shape[0] // 2) + pieces.shape[1:])
    return give_back(give_back(pieces, "core"), "x")


def diagonal_moves(to_expert):
    size = lax.axis_size("z")
    for step in range(1, size):
        yield [
            (i * size + i, j * size + i if to_expert else i * size + j)
            for i in range(size)
            for j in [(i + step) % size]
        ]


def body(
    tokens,
    cotangent,
    routes,
    qkv_w,
    qkv_m,
    qkv_v,
    out_w,
    out_m,
    out_v,
    router_w,
    router_m,
    router_v,
    gains,
    gains_m,
    gains_v,
    expert_in,
    in_m,
    in_v,
    expert_out,
    down_m,
    down_v,
):
    rows = tokens.shape[1]
    width = tokens.shape[2]
    spread = lax.axis_size(EXPERT)
    length = rows * spread
    experts = router_w.shape[1]
    owned = expert_in.shape[0]
    part = qkv_w.shape[0]
    own = lax.axis_index(EXPERT)
    deep = lax.axis_size("z")
    sides = lax.axis_size("y")
    heads = HQ // spread
    keys = KVH // spread
    joint = ("x", "core", "z")
    across = lax.axis_size("x")
    at_x, at_core, at_z, at_y = (lax.axis_index(name) for name in ("x", "core", "z", "y"))

    order = jnp.arange(spread, dtype=jnp.int32)
    slots = (at_core - order % 2) % 2 * across + (at_x - order // 2) % across
    order = jnp.arange(deep * sides, dtype=jnp.int32)
    shards = (at_z - order // sides) % deep * sides + (at_y - order % sides) % sides
    order = jnp.arange(sides, dtype=jnp.int32)
    side_slots = (at_y - order) % sides

    def own_columns(start, size):
        return lax.dynamic_slice_in_dim(qkv_w, start + own * size, size, axis=1).astype(low)

    own_w = jnp.concatenate(
        [
            own_columns(0, heads * HD),
            own_columns(HQ * HD, keys * HD),
            own_columns((HQ + KVH) * HD, keys * HD),
        ],
        axis=1,
    )
    columns = own_w.shape[1]
    own_extra = jnp.concatenate(
        [
            router_w.T.astype(low),
            jnp.pad(gains.astype(low), ((0, EXTRA - 2), (0, columns - 2 * part))),
        ],
        axis=1,
    )
    own_w = jnp.concatenate([own_w, own_extra], axis=0)
    w_all = collect(collect(own_w, "y"), "z").reshape(-1, part + EXTRA, columns)
    x_all = collect_expert(tokens[0])
    gate_w = lax.all_gather(expert_in[:, 0].astype(low), "z", axis=1, tiled=True)
    up_w = lax.all_gather(expert_in[:, 1].astype(low), "z", axis=1, tiled=True)
    down_w = lax.all_gather(expert_out.astype(low), "z", axis=1, tiled=True)
    hidden = gate_w.shape[1]
    inner = owned * hidden
    own_out = out_w.astype(low)
    out_part = jnp.where(at_z == own, own_out, jnp.zeros_like(own_out))
    for moves in diagonal_moves(False):
        out_part = out_part + lax.ppermute(own_out, joint, moves)
    out_all = collect(out_part, "y")
    chosen = jnp.any(
        routes[0][:, :, None] == jnp.arange(128, dtype=jnp.int32)[None, None, :], axis=1
    )
    pack_all = collect_group(jnp.concatenate([cotangent[0], chosen.astype(low)], axis=1))

    cosine, sine = rotary_tables(length)
    normed, weight, extra, query, key, value, attended, totals = attend(
        slots, shards, x_all, w_all, cosine, sine, heads, keys
    )
    router = extra[:experts]
    gains_all = extra[EXTRA : EXTRA + 2].astype(high)
    gain_one = gains_all[0]
    gain_two = gains_all[1]
    branch = give_back_expert(project(slots, side_slots, attended, out_all, spread))
    inputs = tokens[0].astype(high)
    middle = inputs + branch.astype(high)
    scale_two = rms_scale(middle)
    norm_two = (middle * scale_two * gain_two).astype(low)
    h_all = collect_group(norm_two)

    first = (own * owned).astype(jnp.int32).reshape(1)
    act, gate_grad, up_grad, logit_grad, down_grad, router_grad = run_experts(
        first, h_all, pack_all, router, gate_w, up_w, down_w
    )

    def to_shards(grad):
        return lax.psum_scatter(
            grad.reshape(owned, hidden, width), "z", scatter_dimension=1, tiled=True
        )

    down_total = to_shards(down_grad)
    flat_gate = gate_w.reshape(inner, width)
    flat_up = up_w.reshape(inner, width)
    rows_grad = back_rows(gate_grad, up_grad, logit_grad, flat_gate, flat_up, router)
    gate_in, up_in = weight_grads(gate_grad, up_grad, h_all)
    gate_total = to_shards(gate_in)
    up_total = to_shards(up_in)
    norm_two_grad = give_back_group(rows_grad).astype(high)
    results = expert_results(act, down_w.reshape(inner, width))
    mixed = give_back_group(results)
    output = (middle + mixed.astype(high)).astype(low)

    out_grad = cotangent[0].astype(high)
    gain_two_grad = jnp.sum(norm_two_grad * middle * scale_two, axis=0, keepdims=True)
    middle_grad = out_grad + norm_back(middle, scale_two, gain_two, norm_two_grad)
    grad_all = collect_expert(middle_grad.astype(low))
    qkv_grad, out_w_grad, norm_one_grad = attend_back(
        slots,
        shards,
        side_slots,
        grad_all,
        x_all,
        out_all,
        weight,
        normed,
        query,
        key,
        value,
        attended,
        totals,
        cosine,
        sine,
        router_grad,
        gain_two_grad,
    )
    norm_one_grad = give_back_expert(norm_one_grad).astype(high)
    scale_one = rms_scale(inputs)
    input_grad = middle_grad + norm_back(inputs, scale_one, gain_one, norm_one_grad)

    qkv_grad = qkv_grad.reshape(deep, sides, part + EXTRA, columns)
    qkv_total = collect_expert(give_back(give_back(qkv_grad, "z"), "y"))
    out_piece = give_back(out_w_grad, "y")
    out_total = out_piece.astype(high)
    for moves in diagonal_moves(False):
        out_total = out_total + lax.ppermute(out_piece, joint, [(b, a) for a, b in moves]).astype(
            high
        )
    out_piece = out_total.astype(low)
    out_total = jnp.where(at_z == own, out_piece, jnp.zeros_like(out_piece))
    for moves in diagonal_moves(True):
        out_total = out_total + lax.ppermute(out_piece, joint, moves)

    rate = 3.0 * D ** (-0.5)
    qkv_new_m, qkv_new_v, qkv_new_w, extra_total = qkv_step(
        rate, slots, qkv_total, qkv_w, qkv_m, qkv_v
    )
    router_total = extra_total[:experts, :part].T
    gains_total = extra_total[:2, part : 2 * part]
    in_total = jnp.stack([gate_total, up_total], axis=1)
    rates = (
        3.0 * (HQ * HD * 8 // length) ** (-0.5),
        3.0 * (4 * D) ** (-0.5),
        0.6,
        rate,
        3.0 * (FF // 16) ** (-0.5),
    )
    decays = (weight_decay, weight_decay, 0.0, weight_decay, weight_decay)
    masters = (out_w, router_w, gains, expert_in, expert_out)
    firsts = (out_m, router_m, gains_m, in_m, down_m)
    seconds = (out_v, router_v, gains_v, in_v, down_v)
    grads = (out_total, router_total, gains_total, in_total, down_total)
    updated = [qkv_new_m, qkv_new_v, qkv_new_w]
    for index in range(5):
        updated.extend(
            adam_step(
                masters[index],
                firsts[index],
                seconds[index],
                grads[index].astype(high),
                rates[index],
                decays[index],
            )
        )
    return (output[None], input_grad[None], *updated)


def solution(mesh):
    spread = mesh.shape["expert"]
    shards = mesh.shape["shard"]
    short = math.isqrt(shards // 2)
    grid = jax.sharding.Mesh(
        mesh.devices.reshape(spread // 2, 2, shards // short, short), ("x", "core", "z", "y")
    )
    in_specs = (
        P(SHARD, EXPERT, None),
        P(SHARD, EXPERT, None),
        P(SHARD, EXPERT, None),
        P(SHARD, None),
        P(SHARD, None),
        P(SHARD, None),
        P(SHARD, None),
        P(SHARD, None),
        P(SHARD, None),
        P(SHARD, None),
        P(SHARD, None),
        P(SHARD, None),
        P(None, SHARD),
        P(None, SHARD),
        P(None, SHARD),
        P(EXPERT, None, SHARD, None),
        P(EXPERT, None, SHARD, None),
        P(EXPERT, None, SHARD, None),
        P(EXPERT, SHARD, None),
        P(EXPERT, SHARD, None),
        P(EXPERT, SHARD, None),
    )
    out_specs = (
        P(SHARD, EXPERT, None),
        P(SHARD, EXPERT, None),
        P(SHARD, None),
        P(SHARD, None),
        P(SHARD, None),
        P(SHARD, None),
        P(SHARD, None),
        P(SHARD, None),
        P(SHARD, None),
        P(SHARD, None),
        P(SHARD, None),
        P(None, SHARD),
        P(None, SHARD),
        P(None, SHARD),
        P(EXPERT, None, SHARD, None),
        P(EXPERT, None, SHARD, None),
        P(EXPERT, None, SHARD, None),
        P(EXPERT, SHARD, None),
        P(EXPERT, SHARD, None),
        P(EXPERT, SHARD, None),
    )
    return jax.shard_map(body, mesh=grid, in_specs=in_specs, out_specs=out_specs, check_vma=False)
```

time: 1230 us -> 456 us (0.37)
  the two profiles are of different devices: /device:TPU:0 before, /device:TPU:8 now
where the time goes in v2:
time: 456 us; the launch traced here: 448 us
  waiting for transfers between devices  162 us (36%)
  Pallas kernels  113 us (25%)
  other arithmetic  73.6 us (16%)
  starting transfers between devices  60.1 us (13%)
  local copies, waits for them, and re-layouts  23.2 us (5%)
  between operations  15.3 us (3%)
    ppermute x40, waiting for transfers between devices, shifted(): lax.ppermute(value, axis, [(j, (j + step) % size) for j in range(size)])  162 us
    ppermute x40, starting transfers between devices, shifted(): lax.ppermute(value, axis, [(j, (j + step) % size) for j in range(size)])  46.7 us
    pallas_call x1, Pallas kernels, run_experts(): pl.pallas_call(experts_kernel, grid=(count // tile,), out_shape=(jax.Shap...  35.6 us
    another operation x22, other arithmetic, collect(): jnp.stack([value] + [shifted(value, axis, step) for step in range(1, size)])  27.8 us
    pallas_call x1, Pallas kernels, attend_back(): pl.pallas_call(functools.partial(attend_back_kernel, heads, keys), out_sh...  19.7 us
    sub x5, other arithmetic, adam_step(): return (new_first, new_second, weight - rate * (update + decay * weight))  15.9 us
    pallas_call x1, Pallas kernels, back_rows(): pl.pallas_call(back_rows_kernel, grid=(count // tile,), out_shape=jax.Sha...  14.8 us
    pallas_call x1, Pallas kernels, attend(): pl.pallas_call(functools.partial(attend_kernel, heads, keys), out_shape=(...  13.9 us
  transfers between devices with their start and end apart: 55, of which 20 were waited for; matrix products, arithmetic and copies ran while one was open for 20% of the time, Pallas kernels for 14%

profile of v2, /device:TPU:8, one launch (start us, length us, event | category | flops | bytes accessed | tf_op | source)
XLA Modules:
  0.0 447.6 jit_solution(3771728409081462177)
XLA Ops:
  23.3 4.2 collective-permute-done
  32.9 3.6 pad_maximum_fusion.17
  48.8 25.3 %collective-permute-done.5 = bf16[2,144,512]{2,1,0:T(8,128)(2,1)S(1)} collective-permute-done((bf16[2,144,512]{2,1,0:T(8,128)(2,1)}, bf16[2,144,512]{2,1,0:T(8,128)(2,1)S(1)}, u32[]{:S(2)}, u32[]{:S(2)}) %collective-permute-start.5) | collective-permute-done | bytes 294944 | tf_op jit(solution)/shard_map/ppermute | solution.py:667
  76.4 9.7 %collective-permute-done.3 = bf16[2,144,512]{2,1,0:T(8,128)(2,1)S(1)} collective-permute-done((bf16[2,144,512]{2,1,0:T(8,128)(2,1)}, bf16[2,144,512]{2,1,0:T(8,128)(2,1)S(1)}, u32[]{:S(2)}, u32[]{:S(2)}) %collective-permute-start.3) | collective-permute-done | bytes 294944 | tf_op jit(solution)/shard_map/ppermute | solution.py:667
  90.9 13.9 %attend.1 = (bf16[1024,1024]{1,0:T(8,128)(2,1)}, bf16[1024,512]{1,0:T(8,128)(2,1)}, bf16[32,1024]{1,0:T(8,128)(2,1)}, bf16[4,1024,64]{2,1,0:T(8,128)(2,1)}, bf16...) custom-call(s32[4]{0:T(128)} %fusion.45.slots, ...), custom_call_target="tpu_custom_call" | custom-call | flops 1879048192 | bytes 12582912 | tf_op jit(solution)/shard_map/attend/pallas_call | solution.py:178
  104.8 3.3 project.1
  114.3 6.3 %collective-permute-done.19 = bf16[128,1152]{1,0:T(8,128)(2,1)} collective-permute-done((bf16[128,1152]{1,0:T(8,128)(2,1)S(1)}, bf16[128,1152]{1,0:T(8,128)(2,1)}, u32[]{:S(2)}, u32[]{:S(2)}) %collective-permute-start.19) | collective-permute-done | bytes 294944 | tf_op jit(solution)/shard_map/ppermute | solution.py:667
  127.2 10.8 %collective-permute-done.20 = bf16[2,128,1152]{2,1,0:T(8,128)(2,1)S(1)} collective-permute-done((bf16[2,128,1152]{2,1,0:T(8,128)(2,1)S(1)}, bf16[2,128,1152]{2,1,0:T(8,128)(2,1)S(1)}, u32[]{:S(2)}, u32[]{:S(2)}) %collective-permute-start.20) | collective-permute-done | bytes 589856 | tf_op jit(solution)/shard_map/ppermute | solution.py:667
  138.8 8.6 %collective-permute-done.11 = bf16[256,1024]{1,0:T(8,128)(2,1)S(1)} collective-permute-done((bf16[256,1024]{1,0:T(8,128)(2,1)S(1)}, bf16[256,1024]{1,0:T(8,128)(2,1)S(1)}, u32[]{:S(2)}, u32[]{:S(2)}) %collective-permute-start.11) | collective-permute-done | bytes 524320 | tf_op jit(solution)/shard_map/ppermute | solution.py:667
  150.2 4.6 %collective-permute-done.14 = bf16[128,1024]{1,0:T(8,128)(2,1)S(1)} collective-permute-done((bf16[128,1024]{1,0:T(8,128)(2,1)S(1)}, bf16[128,1024]{1,0:T(8,128)(2,1)S(1)}, u32[]{:S(2)}, u32[]{:S(2)}) %collective-permute-start.14) | collective-permute-done | bytes 262176 | tf_op jit(solution)/shard_map/ppermute | solution.py:667
  159.1 8.3 %collective-permute-done.15 = bf16[2,128,1024]{2,1,0:T(8,128)(2,1)S(1)} collective-permute-done((bf16[2,128,1024]{2,1,0:T(8,128)(2,1)S(1)}, bf16[2,128,1024]{2,1,0:T(8,128)(2,1)S(1)}, u32[]{:S(2)}, u32[]{:S(2)}) %collective-permute-start.15) | collective-permute-done | bytes 524320 | tf_op jit(solution)/shard_map/ppermute | solution.py:667
  170.8 4.5 %pad_maximum_fusion = bf16[2,1024,1152]{2,1,0:T(8,128)(2,1)} fusion(bf16[1,1024,1152]{2,1,0:T(8,128)(2,1)} %bitcast.45, bf16[1,1024,1152]{2,1,0:T(8,128)(2,1)S(1)} %get-tuple-element.86), kind=kLoop, calls=%fused_computation | loop fusion | flops 2359296 | bytes 9437184 | tf_op jit(solution)/shard_map/stack | solution.py:672
  175.3 4.0 pad_maximum_fusion.1
  179.3 35.6 %experts.1 = (bf16[2048,1024]{1,0:T(8,128)(2,1)}, bf16[2048,1024]{1,0:T(8,128)(2,1)}, bf16[2048,1024]{1,0:T(8,128)(2,1)}, bf16[2048,16]{1,0:T(8,128)(2,1)}, bf16...) custom-call(s32[1]{0:T(128)} %bitcast.17.first, bf16[2048,1024]{1,0:T(8,128)(2,1)} %bitcast.185, ...), custom_call_target="tpu_custom_call" | custom-call | flops 17179869184 | bytes 31457280 | tf_op jit(solution)/shard_map/experts/pallas_call | solution.py:312
  214.9 13.2 %weight_grads.1 = (bf16[1024,1024]{1,0:T(8,128)(2,1)}, bf16[1024,1024]{1,0:T(8,128)(2,1)}) custom-call(bf16[2048,1024]{1,0:T(8,128)(2,1)} %get-tuple-element.46.gate_grad_ref, bf16[2048,1024]{1,0:T(8,128)(2,1)} %get-tuple-element.47.up_grad_ref, bf16[2048,1024]{1,0:T(8,128)(2,1)} %bitcast.186), custom_call_target="tpu_custom_call" | custom-call | flops 8589934592 | bytes 16777216 | tf_op jit(solution)/shard_map/weight_grads/pallas_call | solution.py:395
  228.1 14.8 %back_rows.1 = bf16[2048,1024]{1,0:T(8,128)(2,1)} custom-call(bf16[2048,1024]{1,0:T(8,128)(2,1)} %get-tuple-element.46.gate_grad_ref, bf16[2048,1024]{1,0:T(8,128)(2,1)} %get-tuple-element.47.up_grad_ref, bf16[2048,16]{1,0:T(8,128)(2,1)} %get-tuple-element.48.logit_ref, bf16[1024,1024]{1,0:T(8,128)(2,1)} %bitcast.233, bf16[1024,1024]{1,0:T(8,128)(2,1)} %bitcast.235, ...), custom_call_target="tpu_custom_call" | custom-call | flops 8589934592 | bytes 16777216 | tf_op jit(solution)/shard_map/back_rows/pallas_call | solution.py:365
  246.6 8.4 %expert_results.1 = bf16[2048,1024]{1,0:T(8,128)(2,1)} custom-call(bf16[2048,1024]{1,0:T(8,128)(2,1)} %get-tuple-element.45.act_ref, bf16[1024,1024]{1,0:T(8,128)(2,1)} %bitcast.236), custom_call_target="tpu_custom_call" | custom-call | flops 4294967296 | bytes 10485760 | tf_op jit(solution)/shard_map/expert_results/pallas_call | solution.py:421
  264.3 12.1 %collective-permute-done.30 = bf16[2,128,1024]{2,1,0:T(8,128)(2,1)S(1)} collective-permute-done((bf16[2,128,1024]{2,1,0:T(8,128)(2,1)S(1)}, bf16[2,128,1024]{2,1,0:T(8,128)(2,1)S(1)}, u32[]{:S(2)}, u32[]{:S(2)}) %collective-permute-start.30) | collective-permute-done | bytes 524320 | tf_op jit(solution)/shard_map/ppermute | solution.py:667
  280.1 4.6 %collective-permute-done.31 = bf16[128,1024]{1,0:T(8,128)(2,1)S(1)} collective-permute-done((bf16[128,1024]{1,0:T(8,128)(2,1)S(1)}, bf16[128,1024]{1,0:T(8,128)(2,1)S(1)}, u32[]{:S(2)}, u32[]{:S(2)}) %collective-permute-start.31) | collective-permute-done | bytes 262176 | tf_op jit(solution)/shard_map/ppermute | solution.py:667
  292.2 9.7 %collective-permute-done.32 = bf16[256,1024]{1,0:T(8,128)(2,1)} collective-permute-done((bf16[256,1024]{1,0:T(8,128)(2,1)S(1)}, bf16[256,1024]{1,0:T(8,128)(2,1)}, u32[]{:S(2)}, u32[]{:S(2)}) %collective-permute-start.32) | collective-permute-done | bytes 524320 | tf_op jit(solution)/shard_map/ppermute | solution.py:667
  303.2 7.3 %collective-permute-done.25 = bf16[2,128,1024]{2,1,0:T(8,128)(2,1)S(1)} collective-permute-done((bf16[2,128,1024]{2,1,0:T(8,128)(2,1)}, bf16[2,128,1024]{2,1,0:T(8,128)(2,1)S(1)}, u32[]{:S(2)}, u32[]{:S(2)}) %collective-permute-start.25) | collective-permute-done | bytes 524320 | tf_op jit(solution)/shard_map/ppermute | solution.py:667
  313.6 3.5 collective-permute-done.26
  319.5 19.7 %attend_back.1 = (bf16[8,144,512]{2,1,0:T(8,128)(2,1)}, bf16[2,128,1024]{2,1,0:T(8,128)(2,1)}, bf16[4,256,1024]{2,1,0:T(8,128)(2,1)}) custom-call(s32[4]{0:T(128)} %fusion.45.slots, s32[8]{0:T(128)} %fusion.47.shards, s32[2]{0:T(128)} %and_select_fusion.4.sides, bf16[4,256,1024]{2,1,0:T(8,128)(2,1)} %bitcast.194, bf16[4,256,1024]{2,1,0:T(8,128)(2,1)} %bitcast.191, ...), custom_call_target="tpu_custom_call" | custom-call | flops 4831838208 | bytes 20971520 | tf_op jit(solution)/shard_map/attend_back/pallas_call | solution.py:571
  345.7 4.7 %collective-permute-start.37 = (bf16[2,144,512]{2,1,0:T(8,128)(2,1)S(1)}, bf16[2,144,512]{2,1,0:T(8,128)(2,1)S(1)}, u32[]{:S(2)}, u32[]{:S(2)}) collective-permute-start(bf16[2,144,512]{2,1,0:T(8,128)(2,1)S(1)} %get-tuple-element.100), channel_id=1, source_target_pairs={{0,4},{2,6},{4,0},{6,2},{1,5},{3,7},{5,1},{7,3},{8,12},{10,14},{12... | collective-permute-start | bytes 884744 | tf_op jit(solution)/shard_map/ppermute | solution.py:667
  354.7 16.6 %collective-permute-done.38 = bf16[2,144,512]{2,1,0:T(8,128)(2,1)S(1)} collective-permute-done((bf16[2,144,512]{2,1,0:T(8,128)(2,1)S(1)}, bf16[2,144,512]{2,1,0:T(8,128)(2,1)S(1)}, u32[]{:S(2)}, u32[]{:S(2)}) %collective-permute-start.38) | collective-permute-done | bytes 294944 | tf_op jit(solution)/shard_map/ppermute | solution.py:667
  373.3 12.3 %collective-permute-done.37 = bf16[2,144,512]{2,1,0:T(8,128)(2,1)S(1)} collective-permute-done((bf16[2,144,512]{2,1,0:T(8,128)(2,1)S(1)}, bf16[2,144,512]{2,1,0:T(8,128)(2,1)S(1)}, u32[]{:S(2)}, u32[]{:S(2)}) %collective-permute-start.37) | collective-permute-done | bytes 294944 | tf_op jit(solution)/shard_map/ppermute | solution.py:667
  385.7 8.1 %collective-permute-done.36 = bf16[2,144,512]{2,1,0:T(8,128)(2,1)S(1)} collective-permute-done((bf16[2,144,512]{2,1,0:T(8,128)(2,1)S(1)}, bf16[2,144,512]{2,1,0:T(8,128)(2,1)S(1)}, u32[]{:S(2)}, u32[]{:S(2)}) %collective-permute-start.36) | collective-permute-done | bytes 294944 | tf_op jit(solution)/shard_map/ppermute | solution.py:667
  397.8 6.7 %multiply_subtract_fusion = (f32[4,2,64,1024]{3,2,1,0:T(8,128)}, f32[4,2,64,1024]{3,2,1,0:T(8,128)}, f32[4,2,64,1024]{3,2,1,0:T(8,128)}) fusion(f32[4,2,64,1024]{3,2,1,0:T(8,128)S(1)} %copy-done.5, bf16[4,1,64,1024]{3,2,1,0:T(8,128)(2,1)} %bitcast.214, bf16[4,1,64,1024]{3,2,1,0:T(8,128)(2,1)} %bitcast.215, f32[4,2,64,1024]{3,2,1,0:T(8,128)} %param.38, ...), kind=kLoop, calls=%fused_computation.13 | loop fusion | flops 8912896 | bytes 13631488 | tf_op jit(solution)/shard_map/sub | solution.py:66
  411.6 4.0 multiply_subtract_fusion.1
  416.6 3.3 collective-permute-start.41
  425.7 4.5 %qkv_step.1 = (f32[128,2048]{1,0:T(8,128)}, f32[128,2048]{1,0:T(8,128)}, f32[128,2048]{1,0:T(8,128)}, f32[16,512]{1,0:T(8,128)}) custom-call(s32[4]{0:T(128)} %fusion.45.slots, bf16[4,144,512]{2,1,0:T(8,128)(2,1)} %bitcast.189, f32[128,2048]{1,0:T(8,128)} %w_ref.1, f32[128,2048]{1,0:T(8,128)} %m_ref.1, f32[128,2048]{1,0:T(8,128)} %v_ref.1), custom_call_target="tpu_custom_call" | custom-call | flops 4194304 | bytes 6291456 | tf_op jit(solution)/shard_map/qkv_step/pallas_call | solution.py:652
  432.9 5.3 %collective-permute-done.35 = bf16[256,1024]{1,0:T(8,128)(2,1)S(1)} collective-permute-done((bf16[256,1024]{1,0:T(8,128)(2,1)S(1)}, bf16[256,1024]{1,0:T(8,128)(2,1)S(1)}, u32[]{:S(2)}, u32[]{:S(2)}) %collective-permute-start.35) | collective-permute-done | bytes 524320 | tf_op jit(solution)/shard_map/ppermute | solution.py:667
  (273 shorter events, 130.7 us)
Async XLA Ops:
  7.2 172.1 %all-gather.8.cloned.1.call-start = ((), (), s32[]{:S(2)}) async-start(), calls=%async_computation.7 | async-start | bytes 2621440 | tf_op jit(solution)/shard_map/all_gather | solution.py:791
  10.1 169.3 %all-gather.10.cloned.1.call-start = ((), (), s32[]{:S(2)}) async-start(), calls=%async_computation.8 | async-start | bytes 2621440 | tf_op jit(solution)/shard_map/all_gather | solution.py:792
  10.9 27.9 %collective-permute-start.8 = (bf16[128,1024]{1,0:T(8,128)(2,1)}, bf16[128,1024]{1,0:T(8,128)(2,1)S(1)}, u32[]{:S(2)}, u32[]{:S(2)}) collective-permute-start(bf16[128,1024]{1,0:T(8,128)(2,1)} %convert_element_type.293), channel_id=1, source_target_pairs={{0,6},{10,8},{20,18},{30,28},{1,7},{11,9},{21,19},{31,29}} | collective-permute-start | bytes 786440 | tf_op jit(solution)/shard_map/ppermute | solution.py:799
  11.5 29.8 %collective-permute-start.7 = (bf16[128,1024]{1,0:T(8,128)(2,1)}, bf16[128,1024]{1,0:T(8,128)(2,1)}, u32[]{:S(2)}, u32[]{:S(2)}) collective-permute-start(bf16[128,1024]{1,0:T(8,128)(2,1)} %convert_element_type.293), channel_id=1, source_target_pairs={{0,4},{10,14},{20,16},{30,26},{1,5},{11,15},{21,17},{31,27}} | collective-permute-start | bytes 786440 | tf_op jit(solution)/shard_map/ppermute | solution.py:799
  12.9 31.3 %collective-permute-start.6 = (bf16[128,1024]{1,0:T(8,128)(2,1)}, bf16[128,1024]{1,0:T(8,128)(2,1)}, u32[]{:S(2)}, u32[]{:S(2)}) collective-permute-start(bf16[128,1024]{1,0:T(8,128)(2,1)} %convert_element_type.293), channel_id=1, source_target_pairs={{0,2},{10,12},{20,22},{30,24},{1,3},{11,13},{21,23},{31,25}} | collective-permute-start | bytes 786440 | tf_op jit(solution)/shard_map/ppermute | solution.py:799
  16.4 162.9 %all-gather.6.cloned.1.call-start = ((), (), s32[]{:S(2)}) async-start(), calls=%async_computation.3 | async-start | bytes 2621440 | tf_op jit(solution)/shard_map/all_gather | solution.py:793
  19.0 17.5 %collective-permute-start.2 = (bf16[144,512]{1,0:T(8,128)(2,1)}, bf16[144,512]{1,0:T(8,128)(2,1)}, u32[]{:S(2)}, u32[]{:S(2)}) collective-permute-start(bf16[144,512]{1,0:T(8,128)(2,1)} %fusion.41), channel_id=1, source_target_pairs={{0,1},{1,0},{2,3},{3,2},{4,5},{5,4},{6,7},{7,6},{8,9},{9,8},{10,11... | collective-permute-start | bytes 442376 | tf_op jit(solution)/shard_map/ppermute | solution.py:667
  30.4 57.7 %collective-permute-start.1 = (bf16[2,256,1024]{2,1,0:T(8,128)(2,1)}, bf16[2,256,1024]{2,1,0:T(8,128)(2,1)}, u32[]{:S(2)}, u32[]{:S(2)}) collective-permute-start(bf16[2,256,1024]{2,1,0:T(8,128)(2,1)} %get-tuple-element.110), channel_id=1, source_target_pairs={{0,8},{8,0},{1,9},{9,1},{2,10},{10,2},{3,11},{11,3},{4,12},{12,4},... | collective-permute-start | bytes 3145736 | tf_op jit(solution)/shard_map/ppermute | solution.py:667
  38.1 36.0 %collective-permute-start.5 = (bf16[2,144,512]{2,1,0:T(8,128)(2,1)}, bf16[2,144,512]{2,1,0:T(8,128)(2,1)S(1)}, u32[]{:S(2)}, u32[]{:S(2)}) collective-permute-start(bf16[2,144,512]{2,1,0:T(8,128)(2,1)} %get-tuple-element.128), channel_id=1, source_target_pairs={{0,6},{2,0},{4,2},{6,4},{1,7},{3,1},{5,3},{7,5},{8,14},{10,8},{12,... | collective-permute-start | bytes 884744 | tf_op jit(solution)/shard_map/ppermute | solution.py:667
  38.8 37.6 %collective-permute-start.4 = (bf16[2,144,512]{2,1,0:T(8,128)(2,1)}, bf16[2,144,512]{2,1,0:T(8,128)(2,1)S(1)}, u32[]{:S(2)}, u32[]{:S(2)}) collective-permute-start(bf16[2,144,512]{2,1,0:T(8,128)(2,1)} %get-tuple-element.128), channel_id=1, source_target_pairs={{0,4},{2,6},{4,0},{6,2},{1,5},{3,7},{5,1},{7,3},{8,12},{10,14},{12... | collective-permute-start | bytes 884744 | tf_op jit(solution)/shard_map/ppermute | solution.py:667
  41.3 44.7 %collective-permute-start.3 = (bf16[2,144,512]{2,1,0:T(8,128)(2,1)}, bf16[2,144,512]{2,1,0:T(8,128)(2,1)S(1)}, u32[]{:S(2)}, u32[]{:S(2)}) collective-permute-start(bf16[2,144,512]{2,1,0:T(8,128)(2,1)} %get-tuple-element.128), channel_id=1, source_target_pairs={{0,2},{2,4},{4,6},{6,0},{1,3},{3,5},{5,7},{7,1},{8,10},{10,12},{12... | collective-permute-start | bytes 884744 | tf_op jit(solution)/shard_map/ppermute | solution.py:667
  45.4 41.9 %collective-permute-start.9 = (bf16[128,1024]{1,0:T(8,128)(2,1)S(1)}, bf16[128,1024]{1,0:T(8,128)(2,1)S(1)}, u32[]{:S(2)}, u32[]{:S(2)}) collective-permute-start(bf16[128,1024]{1,0:T(8,128)(2,1)S(1)} %add_add_fusion.1), channel_id=1, source_target_pairs={{0,1},{1,0},{2,3},{3,2},{4,5},{5,4},{6,7},{7,6},{8,9},{9,8},{10,11... | collective-permute-start | bytes 786440 | tf_op jit(solution)/shard_map/ppermute | solution.py:667
  114.0 283.8 %reduce-scatter.6.cloned.1.call-start = ((), (), s32[]{:S(2)}) async-start(), calls=%async_computation.5 | async-start | bytes 2621440 | tf_op jit(solution)/shard_map/reduce_scatter | solution.py:827
  121.7 16.3 %collective-permute-start.20 = (bf16[2,128,1152]{2,1,0:T(8,128)(2,1)S(1)}, bf16[2,128,1152]{2,1,0:T(8,128)(2,1)S(1)}, u32[]{:S(2)}, u32[]{:S(2)}) collective-permute-start(bf16[2,128,1152]{2,1,0:T(8,128)(2,1)S(1)} %get-tuple-element.116), channel_id=1, source_target_pairs={{0,16},{16,0},{1,17},{17,1},{2,18},{18,2},{3,19},{19,3},{4,20},{20... | collective-permute-start | bytes 1769480 | tf_op jit(solution)/shard_map/ppermute | solution.py:667
  121.9 28.1 %collective-permute-start.18 = (bf16[2,128,1152]{2,1,0:T(8,128)(2,1)S(1)}, bf16[2,128,1152]{2,1,0:T(8,128)(2,1)S(1)}, u32[]{:S(2)}, u32[]{:S(2)}) collective-permute-start(bf16[2,128,1152]{2,1,0:T(8,128)(2,1)S(1)} %get-tuple-element.112), channel_id=1, source_target_pairs={{0,1},{1,0},{2,3},{3,2},{4,5},{5,4},{6,7},{7,6},{8,9},{9,8},{10,11... | collective-permute-start | bytes 1769480 | tf_op jit(solution)/shard_map/ppermute | solution.py:667
  125.2 22.2 %collective-permute-start.11 = (bf16[256,1024]{1,0:T(8,128)(2,1)S(1)}, bf16[256,1024]{1,0:T(8,128)(2,1)S(1)}, u32[]{:S(2)}, u32[]{:S(2)}) collective-permute-start(bf16[256,1024]{1,0:T(8,128)(2,1)S(1)} %slice_bitcast_fusion.2), channel_id=1, source_target_pairs={{0,16},{16,0},{1,17},{17,1},{2,18},{18,2},{3,19},{19,3},{4,20},{20... | collective-permute-start | bytes 1572872 | tf_op jit(solution)/shard_map/ppermute | solution.py:667
  228.1 169.7 %reduce-scatter.4.cloned.1.call-start = ((), (), s32[]{:S(2)}) async-start(), calls=%async_computation.4 | async-start | bytes 2621440 | tf_op jit(solution)/shard_map/reduce_scatter | solution.py:827
  258.2 20.9 %collective-permute-start.22 = (bf16[1024,1024]{1,0:T(8,128)(2,1)}, bf16[1024,1024]{1,0:T(8,128)(2,1)S(1)}, u32[]{:S(2)}, u32[]{:S(2)}) collective-permute-start(bf16[1024,1024]{1,0:T(8,128)(2,1)} %slice.238), channel_id=1, source_target_pairs={{0,8},{8,0},{1,9},{9,1},{2,10},{10,2},{3,11},{11,3},{4,12},{12,4},... | collective-permute-start | bytes 6291464 | tf_op jit(solution)/shard_map/ppermute | solution.py:667
  258.2 153.4 %reduce-scatter.8.cloned.1.call-start = ((), (), s32[]{:S(2)}) async-start(), calls=%async_computation.6 | async-start | bytes 2621440 | tf_op jit(solution)/shard_map/reduce_scatter | solution.py:827
  262.8 14.6 %collective-permute-start.28 = (bf16[2,128,1024]{2,1,0:T(8,128)(2,1)S(1)}, bf16[2,128,1024]{2,1,0:T(8,128)(2,1)S(1)}, u32[]{:S(2)}, u32[]{:S(2)}) collective-permute-start(bf16[2,128,1024]{2,1,0:T(8,128)(2,1)S(1)} %bitcast.212), channel_id=1, source_target_pairs={{0,1},{1,0},{2,3},{3,2},{4,5},{5,4},{6,7},{7,6},{8,9},{9,8},{10,11... | collective-permute-start | bytes 1572872 | tf_op jit(solution)/shard_map/ppermute | solution.py:667
  286.9 15.0 %collective-permute-start.32 = (bf16[256,1024]{1,0:T(8,128)(2,1)S(1)}, bf16[256,1024]{1,0:T(8,128)(2,1)}, u32[]{:S(2)}, u32[]{:S(2)}) collective-permute-start(bf16[256,1024]{1,0:T(8,128)(2,1)S(1)} %fusion.66), channel_id=1, source_target_pairs={{0,16},{16,0},{1,17},{17,1},{2,18},{18,2},{3,19},{19,3},{4,20},{20... | collective-permute-start | bytes 1572872 | tf_op jit(solution)/shard_map/ppermute | solution.py:667
  289.5 21.0 %collective-permute-start.25 = (bf16[2,128,1024]{2,1,0:T(8,128)(2,1)}, bf16[2,128,1024]{2,1,0:T(8,128)(2,1)S(1)}, u32[]{:S(2)}, u32[]{:S(2)}) collective-permute-start(bf16[2,128,1024]{2,1,0:T(8,128)(2,1)} %bitcast.55), channel_id=1, source_target_pairs={{0,16},{16,0},{1,17},{17,1},{2,18},{18,2},{3,19},{19,3},{4,20},{20... | collective-permute-start | bytes 1572872 | tf_op jit(solution)/shard_map/ppermute | solution.py:667
  290.7 21.7 %collective-permute-start.23 = (bf16[2,128,1024]{2,1,0:T(8,128)(2,1)}, bf16[2,128,1024]{2,1,0:T(8,128)(2,1)S(1)}, u32[]{:S(2)}, u32[]{:S(2)}) collective-permute-start(bf16[2,128,1024]{2,1,0:T(8,128)(2,1)} %bitcast.211), channel_id=1, source_target_pairs={{0,1},{1,0},{2,3},{3,2},{4,5},{5,4},{6,7},{7,6},{8,9},{9,8},{10,11... | collective-permute-start | bytes 1572872 | tf_op jit(solution)/shard_map/ppermute | solution.py:667
  303.1 14.8 %collective-permute-start.33 = (bf16[2,256,1024]{2,1,0:T(8,128)(2,1)S(1)}, bf16[2,256,1024]{2,1,0:T(8,128)(2,1)S(1)}, u32[]{:S(2)}, u32[]{:S(2)}) collective-permute-start(bf16[2,256,1024]{2,1,0:T(8,128)(2,1)S(1)} %get-tuple-element.104), channel_id=1, source_target_pairs={{0,8},{8,0},{1,9},{9,1},{2,10},{10,2},{3,11},{11,3},{4,12},{12,4},... | collective-permute-start | bytes 3145736 | tf_op jit(solution)/shard_map/ppermute | solution.py:667
  313.3 37.1 %collective-permute-start.24 = (bf16[128,1024]{1,0:T(8,128)(2,1)}, bf16[128,1024]{1,0:T(8,128)(2,1)S(1)}, u32[]{:S(2)}, u32[]{:S(2)}) collective-permute-start(bf16[128,1024]{1,0:T(8,128)(2,1)} %slice_bitcast_fusion.10), channel_id=1, source_target_pairs={{0,16},{16,0},{1,17},{17,1},{2,18},{18,2},{3,19},{19,3},{4,20},{20... | collective-permute-start | bytes 786440 | tf_op jit(solution)/shard_map/ppermute | solution.py:667
  343.2 28.1 %collective-permute-start.38 = (bf16[2,144,512]{2,1,0:T(8,128)(2,1)S(1)}, bf16[2,144,512]{2,1,0:T(8,128)(2,1)S(1)}, u32[]{:S(2)}, u32[]{:S(2)}) collective-permute-start(bf16[2,144,512]{2,1,0:T(8,128)(2,1)S(1)} %get-tuple-element.99), channel_id=1, source_target_pairs={{0,2},{2,4},{4,6},{6,0},{1,3},{3,5},{5,7},{7,1},{8,10},{10,12},{12... | collective-permute-start | bytes 884744 | tf_op jit(solution)/shard_map/ppermute | solution.py:667
  345.7 40.0 %collective-permute-start.37 = (bf16[2,144,512]{2,1,0:T(8,128)(2,1)S(1)}, bf16[2,144,512]{2,1,0:T(8,128)(2,1)S(1)}, u32[]{:S(2)}, u32[]{:S(2)}) collective-permute-start(bf16[2,144,512]{2,1,0:T(8,128)(2,1)S(1)} %get-tuple-element.100), channel_id=1, source_target_pairs={{0,4},{2,6},{4,0},{6,2},{1,5},{3,7},{5,1},{7,3},{8,12},{10,14},{12... | collective-permute-start | bytes 884744 | tf_op jit(solution)/shard_map/ppermute | solution.py:667
  350.4 43.3 %collective-permute-start.36 = (bf16[2,144,512]{2,1,0:T(8,128)(2,1)S(1)}, bf16[2,144,512]{2,1,0:T(8,128)(2,1)S(1)}, u32[]{:S(2)}, u32[]{:S(2)}) collective-permute-start(bf16[2,144,512]{2,1,0:T(8,128)(2,1)S(1)} %get-tuple-element.98), channel_id=1, source_target_pairs={{0,6},{2,0},{4,2},{6,4},{1,7},{3,1},{5,3},{7,5},{8,14},{10,8},{12,... | collective-permute-start | bytes 884744 | tf_op jit(solution)/shard_map/ppermute | solution.py:667
  352.0 53.8 %collective-permute-start.45 = (bf16[128,1024]{1,0:T(8,128)(2,1)}, bf16[128,1024]{1,0:T(8,128)(2,1)}, u32[]{:S(2)}, u32[]{:S(2)}) collective-permute-start(bf16[128,1024]{1,0:T(8,128)(2,1)} %fusion.27), channel_id=1, source_target_pairs={{6,0},{8,10},{18,20},{28,30},{7,1},{9,11},{19,21},{29,31}} | collective-permute-start | bytes 786440 | tf_op jit(solution)/shard_map/ppermute | solution.py:875
  353.4 52.4 %collective-permute-start.44 = (bf16[128,1024]{1,0:T(8,128)(2,1)}, bf16[128,1024]{1,0:T(8,128)(2,1)}, u32[]{:S(2)}, u32[]{:S(2)}) collective-permute-start(bf16[128,1024]{1,0:T(8,128)(2,1)} %fusion.27), channel_id=1, source_target_pairs={{4,0},{14,10},{16,20},{26,30},{5,1},{15,11},{17,21},{27,31}} | collective-permute-start | bytes 786440 | tf_op jit(solution)/shard_map/ppermute | solution.py:875
  371.4 34.4 %collective-permute-start.43 = (bf16[128,1024]{1,0:T(8,128)(2,1)}, bf16[128,1024]{1,0:T(8,128)(2,1)}, u32[]{:S(2)}, u32[]{:S(2)}) collective-permute-start(bf16[128,1024]{1,0:T(8,128)(2,1)} %fusion.27), channel_id=1, source_target_pairs={{2,0},{12,10},{22,20},{24,30},{3,1},{13,11},{23,21},{25,31}} | collective-permute-start | bytes 786440 | tf_op jit(solution)/shard_map/ppermute | solution.py:875
  405.6 16.9 %collective-permute-start.34 = (bf16[2,256,1024]{2,1,0:T(8,128)(2,1)}, bf16[2,256,1024]{2,1,0:T(8,128)(2,1)}, u32[]{:S(2)}, u32[]{:S(2)}) collective-permute-start(bf16[2,256,1024]{2,1,0:T(8,128)(2,1)} %slice.213), channel_id=1, source_target_pairs={{0,8},{8,0},{1,9},{9,1},{2,10},{10,2},{3,11},{11,3},{4,12},{12,4},... | collective-permute-start | bytes 3145736 | tf_op jit(solution)/shard_map/ppermute | solution.py:667
  (68 other events, 1035.1 us)
Sparse Core Ops, SparseCore 0:
  10.2 72.8 all-gather.7
  85.2 46.4 all-gather.9
  133.2 44.6 all-gather.5
  228.2 44.2 reduce-scatter.5
  274.7 42.0 reduce-scatter.3
  319.0 64.8 reduce-scatter.7
